TPU v7x, 512 devices: a whole 4x4x16 slice. The times are simulated.
512 devices in a mesh: gx: 8 (over x, z_hi), gy: 4 (over y), gz: 16 (over z_lo, core).
Axes of the slice: x: 4, y: 4, z: 16 (z_hi: 2, z_lo: 8; z = z_hi * 8 + z_lo), core: 2. Of those that a mesh axis runs over, the one named last changes fastest.
Arguments:
- volume: float32 [128, 128, 1024], P('gz', 'gx', 'gy'), may hold values from -10 to 10
Outputs:
- diffused: float32 [128, 128, 1024], P('gz', 'gx', 'gy')
All inputs are finite; a program needn't handle non-finite values.
Results may differ from a plain program's by a relative error of at most 0.0003.
Values sent between devices are 32-bit elements; how exact they have to be, the bound alone decides.
A program may use at most 64 MiB of HBM per device.

v0:
```python
import jax
import jax.numpy as jnp
from jax import lax
from jax.sharding import PartitionSpec as P

kernel_taps = (0.41111229, 0.8007374, 1.0, 0.8007374, 0.41111229)
time_step = 3000.0
contrast = 0.1


def extended(shard, sides, width):
    for axis, dim in sides:
        peers, length = (lax.axis_size(axis), shard.shape[dim])
        up = [(i, (i + 1) % peers) for i in range(peers - 1)]
        down = [(j, i) for i, j in up]
        last = lax.slice_in_dim(shard, length - width, length, axis=dim)
        leading = lax.slice_in_dim(shard, 0, width, axis=dim)
        before = lax.ppermute(last, axis, up)
        after = lax.ppermute(leading, axis, down)
        shard = jnp.concatenate([before, shard, after], axis=dim)
    return shard


def blur_valid(values, first_dim):
    weight_sum = sum(kernel_taps)
    for axis_dim in range(first_dim, first_dim + 3):
        out_size = values.shape[axis_dim] - 4
        blurred = kernel_taps[0] / weight_sum * lax.slice_in_dim(values, 0, out_size, axis=axis_dim)
        for offset in range(1, 5):
            blurred = blurred + kernel_taps[offset] / weight_sum * lax.slice_in_dim(
                values, offset, offset + out_size, axis=axis_dim
            )
        values = blurred
    return values


def gradients(values, first_dim):
    result = []
    for axis_dim in range(first_dim, first_dim + 3):
        cropped = values
        for other_dim in range(first_dim, first_dim + 3):
            if other_dim != axis_dim:
                cropped = lax.slice_in_dim(cropped, 1, cropped.shape[other_dim] - 1, axis=other_dim)
        length = cropped.shape[axis_dim] - 2
        forward = lax.slice_in_dim(cropped, 2, length + 2, axis=axis_dim)
        behind = lax.slice_in_dim(cropped, 0, length, axis=axis_dim)
        result.append((forward - behind) * 0.5)
    return result


def shifted(values, stride, axis_dim, fill_value):
    length = values.shape[axis_dim]
    if abs(stride) >= length:
        return jnp.full(values.shape, fill_value, values.dtype)
    pad_shape = list(values.shape)
    pad_shape[axis_dim] = abs(stride)
    padding = jnp.full(tuple(pad_shape), fill_value, values.dtype)
    if stride > 0:
        return jnp.concatenate(
            [padding, lax.slice_in_dim(values, 0, length - stride, axis=axis_dim)], axis=axis_dim
        )
    return jnp.concatenate(
        [lax.slice_in_dim(values, -stride, length, axis=axis_dim), padding], axis=axis_dim
    )


def every_other(values, first_row, axis_dim):
    return lax.slice_in_dim(values, first_row, values.shape[axis_dim], stride=2, axis=axis_dim)


def reduce_solve(sub_diag, main_diag, super_diag, right_sides, axis_dim):
    length = main_diag.shape[axis_dim]
    if length == 1:
        return [right_side / main_diag for right_side in right_sides]
    even_sub = every_other(sub_diag, 0, axis_dim)
    odd_sub = every_other(sub_diag, 1, axis_dim)
    even_main = every_other(main_diag, 0, axis_dim)
    odd_main = every_other(main_diag, 1, axis_dim)
    even_super = every_other(super_diag, 0, axis_dim)
    odd_super = every_other(super_diag, 1, axis_dim)
    even_sides = [every_other(right_side, 0, axis_dim) for right_side in right_sides]
    odd_sides = [every_other(right_side, 1, axis_dim) for right_side in right_sides]
    lower_factor = -even_sub / shifted(odd_main, 1, axis_dim, 1.0)
    upper_factor = -even_super / odd_main
    reduced = reduce_solve(
        lower_factor * shifted(odd_sub, 1, axis_dim, 0.0),
        even_main + lower_factor * shifted(odd_super, 1, axis_dim, 0.0) + upper_factor * odd_sub,
        upper_factor * odd_super,
        [
            even_side + lower_factor * shifted(odd_side, 1, axis_dim, 0.0) + upper_factor * odd_side
            for even_side, odd_side in zip(even_sides, odd_sides)
        ],
        axis_dim,
    )
    result = []
    for even_part, odd_side in zip(reduced, odd_sides):
        odd_part = (
            odd_side - odd_sub * even_part - odd_super * shifted(even_part, -1, axis_dim, 0.0)
        ) / odd_main
        joined = jnp.stack([even_part, odd_part], axis=axis_dim + 1)
        joined_shape = list(even_part.shape)
        joined_shape[axis_dim] = 2 * joined_shape[axis_dim]
        result.append(joined.reshape(tuple(joined_shape)))
    return result


def face_pairs(diffusivity, axis_dim, position, device_count):
    cropped = diffusivity
    for other_dim in range(3):
        if other_dim != axis_dim:
            cropped = lax.slice_in_dim(cropped, 1, cropped.shape[other_dim] - 1, axis=other_dim)
    length = cropped.shape[axis_dim] - 2
    centre = lax.slice_in_dim(cropped, 1, length + 1, axis=axis_dim)
    following = lax.slice_in_dim(cropped, 2, length + 2, axis=axis_dim)
    before = lax.slice_in_dim(cropped, 0, length, axis=axis_dim)
    face_up = (centre + following) * 0.5
    face_down = (before + centre) * 0.5
    global_index = position * length + lax.broadcasted_iota(jnp.int32, face_up.shape, axis_dim)
    face_up = jnp.where(global_index < length * device_count - 1, face_up, 0.0)
    face_down = jnp.where(global_index > 0, face_down, 0.0)
    return (face_up, face_down)


def line_solve(values, face_up, axis_dim, stiffness):
    face_down = shifted(face_up, 1, axis_dim, 0.0)
    return reduce_solve(
        -stiffness * face_down,
        1.0 + stiffness * (face_down + face_up),
        -stiffness * face_up,
        [values],
        axis_dim,
    )[0]


def body(volume):
    stiffness = 3.0 * time_step
    positions = (lax.axis_index("gz"), lax.axis_index("gx"), lax.axis_index("gy"))
    counts = (lax.axis_size("gz"), lax.axis_size("gx"), lax.axis_size("gy"))
    widened = extended(volume, (("gx", 1), ("gy", 2), ("gz", 0)), 3)
    blurred = blur_valid(widened, 0)
    squares = jnp.stack([slope * slope for slope in gradients(blurred, 0)])
    square_halo = extended(squares, (("gx", 2), ("gy", 3), ("gz", 1)), 3)
    tensor = blur_valid(square_halo, 1)
    diffusivity = 1.0 / (1.0 + tensor / (contrast * contrast))
    up_z, down_z = face_pairs(diffusivity[0], 0, positions[0], counts[0])
    up_x, down_x = face_pairs(diffusivity[1], 1, positions[1], counts[1])
    up_y, down_y = face_pairs(diffusivity[2], 2, positions[2], counts[2])
    lines_x = (lambda pieces: line_solve(pieces[0], pieces[1], 1, stiffness))(
        (
            lax.all_to_all(volume, "gx", split_axis=0, concat_axis=1, tiled=True),
            lax.all_to_all(up_x, "gx", split_axis=0, concat_axis=1, tiled=True),
        )
    )
    solved_x = lax.all_to_all(lines_x, "gx", split_axis=1, concat_axis=0, tiled=True)
    lines_y = (lambda pieces: line_solve(pieces[0], pieces[1], 2, stiffness))(
        (
            lax.all_to_all(volume, "gy", split_axis=0, concat_axis=2, tiled=True),
            lax.all_to_all(up_y, "gy", split_axis=0, concat_axis=2, tiled=True),
        )
    )
    solved_y = lax.all_to_all(lines_y, "gy", split_axis=2, concat_axis=0, tiled=True)
    lines_z = (lambda pieces: line_solve(pieces[0], pieces[1], 0, stiffness))(
        (
            lax.all_to_all(volume, "gz", split_axis=1, concat_axis=0, tiled=True),
            lax.all_to_all(up_z, "gz", split_axis=1, concat_axis=0, tiled=True),
        )
    )
    solved_z = lax.all_to_all(lines_z, "gz", split_axis=0, concat_axis=1, tiled=True)
    summed = solved_x + solved_y + solved_z
    return summed / 3.0


def solution(mesh):
    return jax.shard_map(
        body,
        mesh=mesh,
        in_specs=(P("gz", "gx", "gy"),),
        out_specs=P("gz", "gx", "gy"),
        check_vma=False,
    )
```

profile of v0, /device:TPU:1, one launch (start us, length us, event | category | flops | bytes accessed | tf_op | source)
XLA Modules:
  0.0 376.5 jit_solution(18184623434700100287)
XLA Ops:
  0.0 1.6 copy.184
  2.4 16.3 %collective-permute-start = (f32[8,3,256]{2,0,1:T(8,128)S(1)}, f32[8,3,256]{2,0,1:T(8,128)S(1)}, u32[]{:S(2)}, u32[]{:S(2)}) collective-permute-start(f32[8,3,256]{2,0,1:T(8,128)S(1)} %get-tuple-element.90), channel_id=1, source_target_pairs={{0,64},{64,128},{128,192},{192,256},{256,320},{320,384},{384,448},... | collective-permute-start | bytes 73736 | tf_op jit(solution)/shard_map/ppermute | solution.py:18
  21.0 11.0 %collective-permute-done.1 = f32[8,3,256]{2,0,1:T(8,128)S(1)} collective-permute-done((f32[8,3,256]{2,0,1:T(8,128)S(1)}, f32[8,3,256]{2,0,1:T(8,128)S(1)}, u32[]{:S(2)}, u32[]{:S(2)}) %collective-permute-start.1) | collective-permute-done | bytes 24608 | tf_op jit(solution)/shard_map/ppermute | solution.py:19
  32.0 3.2 collective-permute-start.2
  36.8 3.7 collective-permute-done.3
  40.7 6.1 %collective-permute-start.4 = (f32[3,22,262]{2,0,1:T(4,128)S(1)}, f32[3,22,262]{2,0,1:T(4,128)S(1)}, u32[]{:S(2)}, u32[]{:S(2)}) collective-permute-start(f32[3,22,262]{2,0,1:T(4,128)S(1)} %get-tuple-element.62), channel_id=1, source_target_pairs={{0,1},{1,2},{2,3},{3,4},{4,5},{5,6},{6,7},{7,8},{8,9},{9,10},{10,1... | collective-permute-start | bytes 207512 | tf_op jit(solution)/shard_map/ppermute | solution.py:18
  46.8 1.9 collective-permute-start.5
  48.7 3.9 %all-to-all-start.3 = ((f32[8,16,256]{2,1,0:T(8,128)}), f32[8,16,256]{2,1,0:T(8,128)}, u32[]{:S(2)}, u32[]{:S(2)}) async-start(f32[8,16,256]{2,1,0:T(8,128)} %param.1), calls=%async_computation.3 | async-start | bytes 262144 | tf_op jit(solution)/shard_map/all_to_all | solution.py:157
  54.8 3.0 collective-permute-start.6
  59.3 16.2 %collective-permute-done.7 = f32[3,8,3,256]{3,1,2,0:T(8,128)S(1)} collective-permute-done((f32[3,8,3,256]{3,1,2,0:T(8,128)S(1)}, f32[3,8,3,256]{3,1,2,0:T(8,128)S(1)}, u32[]{:S(2)}, u32[]{:S(2)}) %collective-permute-start.7) | collective-permute-done | bytes 73760 | tf_op jit(solution)/shard_map/ppermute | solution.py:19
  75.7 3.7 collective-permute-start.8
  80.7 4.4 %collective-permute-done.8 = f32[3,8,22,3]{3,1,2,0:T(8,128)S(1)} collective-permute-done((f32[3,8,22,3]{3,1,2,0:T(8,128)S(1)}, f32[3,8,22,3]{3,1,2,0:T(8,128)S(1)}, u32[]{:S(2)}, u32[]{:S(2)}) %collective-permute-start.8) | collective-permute-done | bytes 6368 | tf_op jit(solution)/shard_map/ppermute | solution.py:18
  85.1 3.8 %collective-permute-done.9 = f32[3,8,22,3]{3,1,2,0:T(8,128)S(1)} collective-permute-done((f32[3,8,22,3]{3,1,2,0:T(8,128)S(1)}, f32[3,8,22,3]{3,1,2,0:T(8,128)S(1)}, u32[]{:S(2)}, u32[]{:S(2)}) %collective-permute-start.9) | collective-permute-done | bytes 6368 | tf_op jit(solution)/shard_map/ppermute | solution.py:19
  90.3 10.5 %collective-permute-start.10 = (f32[3,3,22,262]{3,1,2,0:T(4,128)}, f32[3,3,22,262]{3,1,2,0:T(4,128)S(1)}, u32[]{:S(2)}, u32[]{:S(2)}) collective-permute-start(f32[3,3,22,262]{3,1,2,0:T(4,128)} %get-tuple-element.47), channel_id=1, source_target_pairs={{0,1},{1,2},{2,3},{3,4},{4,5},{5,6},{6,7},{7,8},{8,9},{9,10},{10,1... | collective-permute-start | bytes 622520 | tf_op jit(solution)/shard_map/ppermute | solution.py:18
  100.8 1.9 collective-permute-start.11
  103.2 8.4 %all-to-all-start = ((f32[8,16,256]{2,1,0:T(8,128)}), f32[8,16,256]{2,1,0:T(8,128)}, u32[]{:S(2)}, u32[]{:S(2)}) async-start(f32[8,16,256]{2,1,0:T(8,128)} %param.1), calls=%async_computation | async-start | bytes 262144 | tf_op jit(solution)/shard_map/all_to_all | solution.py:150
  111.6 2.2 copy.188
  113.8 3.0 slice.1286
  116.8 4.1 %slice.1277 = f32[2,16,512]{1,2,0:T(8,128)} slice(f32[2,16,1024]{1,2,0:T(8,128)} %bitcast.240), slice={[0:2:1], [0:16:1], [0:1024:2]} | slice | bytes 131072 | tf_op jit(solution)/shard_map/slice | solution.py:68
  120.9 3.7 maximum_maximum_fusion
  124.6 2.3 fusion
  130.4 3.3 all-to-all-start.4
  135.7 2.8 all-to-all-done.4
  138.6 8.0 %all-to-all-start.6 = ((f32[8,16,256]{2,0,1:T(8,128)}), f32[8,16,256]{2,0,1:T(8,128)}, u32[]{:S(2)}, u32[]{:S(2)}) async-start(f32[8,16,256]{2,0,1:T(8,128)} %copy.184), calls=%async_computation.6 | async-start | bytes 262144 | tf_op jit(solution)/shard_map/all_to_all | solution.py:164
  146.9 1.6 pad_multiply_fusion
  148.5 3.0 slice.1290
  151.5 4.1 %slice.1283 = f32[2,16,512]{1,2,0:T(8,128)} slice(f32[2,16,1024]{1,2,0:T(8,128)} %get-tuple-element.44), slice={[0:2:1], [0:16:1], [0:1024:2]} | slice | bytes 131072 | tf_op jit(solution)/shard_map/slice | solution.py:68
  155.5 3.0 slice.1294
  158.5 4.1 %slice.1288 = f32[2,16,512]{1,2,0:T(8,128)} slice(f32[2,16,1024]{1,2,0:T(8,128)} %get-tuple-element.46), slice={[0:2:1], [0:16:1], [0:1024:2]} | slice | bytes 131072 | tf_op jit(solution)/shard_map/slice | solution.py:68
  163.4 2.2 slice.1293
  165.6 3.0 multiply_add_fusion.2
  172.7 1.7 slice.1300
  175.5 1.7 slice.1305
  177.2 2.2 multiply_add_fusion.4
  180.4 1.6 slice.1301
  183.0 1.6 slice.1304
  185.6 1.6 slice.1312
  187.2 1.6 slice.1308
  188.8 1.6 slice.1317
  190.4 2.1 multiply_add_fusion.7
  192.5 1.5 slice.1322
  194.0 1.5 slice.1313
  195.5 1.5 slice.1326
  197.1 1.5 slice.1316
  198.6 1.5 slice.1330
  200.1 1.5 slice.1324
  201.6 1.5 slice.1320
  203.2 1.5 slice.1329
  204.7 1.9 multiply_add_fusion.12
  218.2 1.6 multiply_add_fusion.18
  230.0 1.5 multiply_add_fusion.24
  242.0 1.5 multiply_add_fusion.30
  253.8 1.5 multiply_add_fusion.36
  276.0 14.1 %all-to-all-start.1 = ((f32[8,16,256]{2,1,0:T(8,128)}), f32[8,16,256]{2,1,0:T(8,128)S(1)}, u32[]{:S(2)}, u32[]{:S(2)}) async-start(f32[8,16,256]{2,1,0:T(8,128)} %copy.187), calls=%async_computation.1 | async-start | bytes 262144 | tf_op jit(solution)/shard_map/all_to_all | solution.py:151
  293.5 2.1 reshape.133
  297.4 7.1 %all-to-all-done.1 = f32[8,16,256]{2,1,0:T(8,128)S(1)} async-done(((f32[8,16,256]{2,1,0:T(8,128)}), f32[8,16,256]{2,1,0:T(8,128)S(1)}, u32[]{:S(2)}, u32[]{:S(2)}) %all-to-all-start.1) | async-done | bytes 131104 | tf_op jit(solution)/shard_map/all_to_all | solution.py:151
  304.5 13.9 %all-to-all-start.7 = ((f32[8,16,256]{2,0,1:T(8,128)}), f32[8,16,256]{2,0,1:T(8,128)S(1)}, u32[]{:S(2)}, u32[]{:S(2)}) async-start(f32[8,16,256]{2,0,1:T(8,128)} %fusion.30), calls=%async_computation.7 | async-start | bytes 262144 | tf_op jit(solution)/shard_map/all_to_all | solution.py:165
  322.2 8.2 %all-to-all-done.7 = f32[8,16,256]{2,0,1:T(8,128)S(1)} async-done(((f32[8,16,256]{2,0,1:T(8,128)}), f32[8,16,256]{2,0,1:T(8,128)S(1)}, u32[]{:S(2)}, u32[]{:S(2)}) %all-to-all-start.7) | async-done | bytes 131104 | tf_op jit(solution)/shard_map/all_to_all | solution.py:165
  330.4 3.5 all-to-all-start.5
  335.6 2.9 all-to-all-done.5
  338.5 3.4 all-to-all-start.2
  342.9 13.4 %all-to-all-done.2 = f32[1,128,256]{2,0,1:T(1,128)S(1)} async-done(((f32[1,128,256]{2,0,1:T(1,128)}), f32[1,128,256]{2,0,1:T(1,128)S(1)}, u32[]{:S(2)}, u32[]{:S(2)}) %all-to-all-start.2) | async-done | bytes 131104 | tf_op jit(solution)/shard_map/all_to_all | solution.py:154
  356.3 7.4 %all-to-all-start.8 = ((f32[128,1,256]{2,1,0:T(1,128)}), f32[128,1,256]{2,1,0:T(1,128)S(1)}, u32[]{:S(2)}, u32[]{:S(2)}) async-start(f32[128,1,256]{2,1,0:T(1,128)} %bitcast.99), calls=%async_computation.8 | async-start | bytes 262144 | tf_op jit(solution)/shard_map/all_to_all | solution.py:168
  367.1 8.6 %all-to-all-done.8 = f32[128,1,256]{2,1,0:T(1,128)S(1)} async-done(((f32[128,1,256]{2,1,0:T(1,128)}), f32[128,1,256]{2,1,0:T(1,128)S(1)}, u32[]{:S(2)}, u32[]{:S(2)}) %all-to-all-start.8) | async-done | bytes 131104 | tf_op jit(solution)/shard_map/all_to_all | solution.py:168
  (346 shorter events, 103.9 us)
Async XLA Ops:
  2.4 17.6 %collective-permute-start = (f32[8,3,256]{2,0,1:T(8,128)S(1)}, f32[8,3,256]{2,0,1:T(8,128)S(1)}, u32[]{:S(2)}, u32[]{:S(2)}) collective-permute-start(f32[8,3,256]{2,0,1:T(8,128)S(1)} %get-tuple-element.90), channel_id=1, source_target_pairs={{0,64},{64,128},{128,192},{192,256},{256,320},{320,384},{384,448},... | collective-permute-start | bytes 73736 | tf_op jit(solution)/shard_map/ppermute | solution.py:18
  18.7 13.3 %collective-permute-start.1 = (f32[8,3,256]{2,0,1:T(8,128)S(1)}, f32[8,3,256]{2,0,1:T(8,128)S(1)}, u32[]{:S(2)}, u32[]{:S(2)}) collective-permute-start(f32[8,3,256]{2,0,1:T(8,128)S(1)} %get-tuple-element.89), channel_id=1, source_target_pairs={{64,0},{128,64},{192,128},{256,192},{320,256},{384,320},{448,384},... | collective-permute-start | bytes 73736 | tf_op jit(solution)/shard_map/ppermute | solution.py:19
  32.0 4.8 %collective-permute-start.2 = (f32[8,22,3]{2,0,1:T(8,128)S(1)}, f32[8,22,3]{2,0,1:T(8,128)S(1)}, u32[]{:S(2)}, u32[]{:S(2)}) collective-permute-start(f32[8,22,3]{2,0,1:T(8,128)S(1)} %get-tuple-element.70), channel_id=1, source_target_pairs={{0,16},{16,32},{32,48},{1,17},{17,33},{33,49},{2,18},{18,34},{34,5... | collective-permute-start | bytes 6344 | tf_op jit(solution)/shard_map/ppermute | solution.py:18
  35.3 5.3 %collective-permute-start.3 = (f32[8,22,3]{2,0,1:T(8,128)S(1)}, f32[8,22,3]{2,0,1:T(8,128)S(1)}, u32[]{:S(2)}, u32[]{:S(2)}) collective-permute-start(f32[8,22,3]{2,0,1:T(8,128)S(1)} %get-tuple-element.71), channel_id=1, source_target_pairs={{16,0},{32,16},{48,32},{17,1},{33,17},{49,33},{18,2},{34,18},{50,3... | collective-permute-start | bytes 6344 | tf_op jit(solution)/shard_map/ppermute | solution.py:19
  40.7 12.0 %collective-permute-start.4 = (f32[3,22,262]{2,0,1:T(4,128)S(1)}, f32[3,22,262]{2,0,1:T(4,128)S(1)}, u32[]{:S(2)}, u32[]{:S(2)}) collective-permute-start(f32[3,22,262]{2,0,1:T(4,128)S(1)} %get-tuple-element.62), channel_id=1, source_target_pairs={{0,1},{1,2},{2,3},{3,4},{4,5},{5,6},{6,7},{7,8},{8,9},{9,10},{10,1... | collective-permute-start | bytes 207512 | tf_op jit(solution)/shard_map/ppermute | solution.py:18
  46.8 6.3 %collective-permute-start.5 = (f32[3,22,262]{2,0,1:T(4,128)S(1)}, f32[3,22,262]{2,0,1:T(4,128)S(1)}, u32[]{:S(2)}, u32[]{:S(2)}) collective-permute-start(f32[3,22,262]{2,0,1:T(4,128)S(1)} %get-tuple-element.63), channel_id=1, source_target_pairs={{1,0},{2,1},{3,2},{4,3},{5,4},{6,5},{7,6},{8,7},{9,8},{10,9},{11,1... | collective-permute-start | bytes 207512 | tf_op jit(solution)/shard_map/ppermute | solution.py:19
  48.7 54.4 %all-to-all-start.3 = ((f32[8,16,256]{2,1,0:T(8,128)}), f32[8,16,256]{2,1,0:T(8,128)}, u32[]{:S(2)}, u32[]{:S(2)}) async-start(f32[8,16,256]{2,1,0:T(8,128)} %param.1), calls=%async_computation.3 | async-start | bytes 262144 | tf_op jit(solution)/shard_map/all_to_all | solution.py:157
  54.8 4.4 %collective-permute-start.6 = (f32[3,8,3,256]{3,1,2,0:T(8,128)S(1)}, f32[3,8,3,256]{3,1,2,0:T(8,128)S(1)}, u32[]{:S(2)}, u32[]{:S(2)}) collective-permute-start(f32[3,8,3,256]{3,1,2,0:T(8,128)S(1)} %get-tuple-element.58), channel_id=1, source_target_pairs={{0,64},{64,128},{128,192},{192,256},{256,320},{320,384},{384,448},... | collective-permute-start | bytes 221192 | tf_op jit(solution)/shard_map/ppermute | solution.py:18
  57.9 17.6 %collective-permute-start.7 = (f32[3,8,3,256]{3,1,2,0:T(8,128)S(1)}, f32[3,8,3,256]{3,1,2,0:T(8,128)S(1)}, u32[]{:S(2)}, u32[]{:S(2)}) collective-permute-start(f32[3,8,3,256]{3,1,2,0:T(8,128)S(1)} %get-tuple-element.59), channel_id=1, source_target_pairs={{64,0},{128,64},{192,128},{256,192},{320,256},{384,320},{448,384},... | collective-permute-start | bytes 221192 | tf_op jit(solution)/shard_map/ppermute | solution.py:19
  59.3 30.0 %copy-start.3 = (f32[3,8,3,256]{3,1,2,0:T(8,128)}, f32[3,8,3,256]{3,1,2,0:T(8,128)S(1)}, u32[]{:S(2)}) copy-start(f32[3,8,3,256]{3,1,2,0:T(8,128)S(1)} %collective-permute-done.6) | copy-start | bytes 221188
  75.5 13.8 %copy-start.5 = (f32[3,8,3,256]{3,1,2,0:T(8,128)}, f32[3,8,3,256]{3,1,2,0:T(8,128)S(1)}, u32[]{:S(2)}) copy-start(f32[3,8,3,256]{3,1,2,0:T(8,128)S(1)} %collective-permute-done.7) | copy-start | bytes 221188
  75.7 9.4 %collective-permute-start.8 = (f32[3,8,22,3]{3,1,2,0:T(8,128)S(1)}, f32[3,8,22,3]{3,1,2,0:T(8,128)S(1)}, u32[]{:S(2)}, u32[]{:S(2)}) collective-permute-start(f32[3,8,22,3]{3,1,2,0:T(8,128)S(1)} %get-tuple-element.49), channel_id=1, source_target_pairs={{0,16},{16,32},{32,48},{1,17},{17,33},{33,49},{2,18},{18,34},{34,5... | collective-permute-start | bytes 19016 | tf_op jit(solution)/shard_map/ppermute | solution.py:18
  79.4 9.5 %collective-permute-start.9 = (f32[3,8,22,3]{3,1,2,0:T(8,128)S(1)}, f32[3,8,22,3]{3,1,2,0:T(8,128)S(1)}, u32[]{:S(2)}, u32[]{:S(2)}) collective-permute-start(f32[3,8,22,3]{3,1,2,0:T(8,128)S(1)} %get-tuple-element.50), channel_id=1, source_target_pairs={{16,0},{32,16},{48,32},{17,1},{33,17},{49,33},{18,2},{34,18},{50,3... | collective-permute-start | bytes 19016 | tf_op jit(solution)/shard_map/ppermute | solution.py:19
  90.3 30.6 %collective-permute-start.10 = (f32[3,3,22,262]{3,1,2,0:T(4,128)}, f32[3,3,22,262]{3,1,2,0:T(4,128)S(1)}, u32[]{:S(2)}, u32[]{:S(2)}) collective-permute-start(f32[3,3,22,262]{3,1,2,0:T(4,128)} %get-tuple-element.47), channel_id=1, source_target_pairs={{0,1},{1,2},{2,3},{3,4},{4,5},{5,6},{6,7},{7,8},{8,9},{9,10},{10,1... | collective-permute-start | bytes 622520 | tf_op jit(solution)/shard_map/ppermute | solution.py:18
  100.8 20.1 %collective-permute-start.11 = (f32[3,3,22,262]{3,1,2,0:T(4,128)}, f32[3,3,22,262]{3,1,2,0:T(4,128)}, u32[]{:S(2)}, u32[]{:S(2)}) collective-permute-start(f32[3,3,22,262]{3,1,2,0:T(4,128)} %get-tuple-element.48), channel_id=1, source_target_pairs={{1,0},{2,1},{3,2},{4,3},{5,4},{6,5},{7,6},{8,7},{9,8},{10,9},{11,1... | collective-permute-start | bytes 622520 | tf_op jit(solution)/shard_map/ppermute | solution.py:19
  103.2 27.3 %all-to-all-start = ((f32[8,16,256]{2,1,0:T(8,128)}), f32[8,16,256]{2,1,0:T(8,128)}, u32[]{:S(2)}, u32[]{:S(2)}) async-start(f32[8,16,256]{2,1,0:T(8,128)} %param.1), calls=%async_computation | async-start | bytes 262144 | tf_op jit(solution)/shard_map/all_to_all | solution.py:150
  120.9 3.7 copy-start.4
  120.9 3.7 copy-start.6
  130.4 8.1 %all-to-all-start.4 = ((f32[8,16,256]{2,1,0:T(8,128)}), f32[8,16,256]{2,1,0:T(8,128)S(1)}, u32[]{:S(2)}, u32[]{:S(2)}) async-start(f32[8,16,256]{2,1,0:T(8,128)} %copy.189), calls=%async_computation.4 | async-start | bytes 262144 | tf_op jit(solution)/shard_map/all_to_all | solution.py:158
  135.7 10.9 %copy-start.1 = (f32[1,128,256]{2,0,1:T(1,128)}, f32[1,128,256]{2,0,1:T(1,128)S(1)}, u32[]{:S(2)}) copy-start(f32[1,128,256]{2,0,1:T(1,128)S(1)} %all_to_all.106) | copy-start | bytes 393220
  135.7 11.2 %copy-start.7 = (f32[1,64,256]{2,0,1:T(1,128)}, f32[1,64,256]{2,0,1:T(1,128)S(1)}, u32[]{:S(2)}) copy-start(f32[1,64,256]{2,0,1:T(1,128)S(1)} %slice.1195) | copy-start | bytes 196612
  138.6 137.4 %all-to-all-start.6 = ((f32[8,16,256]{2,0,1:T(8,128)}), f32[8,16,256]{2,0,1:T(8,128)}, u32[]{:S(2)}, u32[]{:S(2)}) async-start(f32[8,16,256]{2,0,1:T(8,128)} %copy.184), calls=%async_computation.6 | async-start | bytes 262144 | tf_op jit(solution)/shard_map/all_to_all | solution.py:164
  265.5 9.4 %copy-start = (f32[2,16,128]{1,2,0:T(8,128)S(1)}, f32[2,16,128]{1,2,0:T(8,128)}, u32[]{:S(2)}) copy-start(f32[2,16,128]{1,2,0:T(8,128)} %slice.1308) | copy-start | bytes 49156
  276.0 28.5 %all-to-all-start.1 = ((f32[8,16,256]{2,1,0:T(8,128)}), f32[8,16,256]{2,1,0:T(8,128)S(1)}, u32[]{:S(2)}, u32[]{:S(2)}) async-start(f32[8,16,256]{2,1,0:T(8,128)} %copy.187), calls=%async_computation.1 | async-start | bytes 262144 | tf_op jit(solution)/shard_map/all_to_all | solution.py:151
  293.5 25.4 %copy-start.2 = (f32[1,128,256]{2,0,1:T(1,128)S(1)}, f32[1,128,256]{2,0,1:T(1,128)}, u32[]{:S(2)}) copy-start(f32[1,128,256]{2,0,1:T(1,128)} %copy-done.1) | copy-start | bytes 393220
  293.5 25.4 %slice-start = ((f32[1,64,256]{2,0,1:T(1,128)}), f32[1,63,256]{2,0,1:T(1,128)S(1)}, s32[]{:S(2)}) async-start(f32[1,64,256]{2,0,1:T(1,128)} %copy-done.7), calls=%async_computation.9 | async-start | bytes 129024 | tf_op jit(solution)/shard_map/slice | solution.py:60
  304.5 25.9 %all-to-all-start.7 = ((f32[8,16,256]{2,0,1:T(8,128)}), f32[8,16,256]{2,0,1:T(8,128)S(1)}, u32[]{:S(2)}, u32[]{:S(2)}) async-start(f32[8,16,256]{2,0,1:T(8,128)} %fusion.30), calls=%async_computation.7 | async-start | bytes 262144 | tf_op jit(solution)/shard_map/all_to_all | solution.py:165
  330.4 8.1 %all-to-all-start.5 = ((f32[4,1,8192]{2,1,0:T(1,128)}), f32[4,1,8192]{2,1,0:T(1,128)S(1)}, u32[]{:S(2)}, u32[]{:S(2)}) async-start(f32[4,1,8192]{2,1,0:T(1,128)} %reshape.133), calls=%async_computation.5 | async-start | bytes 262144 | tf_op jit(solution)/shard_map/all_to_all | solution.py:161
  338.5 17.8 %all-to-all-start.2 = ((f32[1,128,256]{2,0,1:T(1,128)}), f32[1,128,256]{2,0,1:T(1,128)S(1)}, u32[]{:S(2)}, u32[]{:S(2)}) async-start(f32[1,128,256]{2,0,1:T(1,128)} %bitcast.24), calls=%async_computation.2 | async-start | bytes 262144 | tf_op jit(solution)/shard_map/all_to_all | solution.py:154
  356.3 19.4 %all-to-all-start.8 = ((f32[128,1,256]{2,1,0:T(1,128)}), f32[128,1,256]{2,1,0:T(1,128)S(1)}, u32[]{:S(2)}, u32[]{:S(2)}) async-start(f32[128,1,256]{2,1,0:T(1,128)} %bitcast.99), calls=%async_computation.8 | async-start | bytes 262144 | tf_op jit(solution)/shard_map/all_to_all | solution.py:168
where the time goes:
time: 382 us; the launch traced here: 376 us
  local copies, waits for them, and re-layouts  132 us (35%)
  starting transfers between devices  118 us (31%)
  waiting for transfers between devices  82.8 us (22%)
  other arithmetic  41.6 us (11%)
    slice x133, local copies, waits for them, and re-layouts, every_other(): lax.slice_in_dim(values, first_row, values.shape[axis_dim], stride=2, axi...  112 us
    ppermute x6, starting transfers between devices, extended(): before = lax.ppermute(last, axis, up)  42.8 us
    ppermute x6, waiting for transfers between devices, extended(): after = lax.ppermute(leading, axis, down)  35.1 us
    add x21, other arithmetic, reduce_solve(): even_side + lower_factor * shifted(odd_side, 1, axis_dim, 0.0)  16.7 us
    all_to_all x1, starting transfers between devices, body(): lax.all_to_all(up_x, 'gx', split_axis=0, concat_axis=1, tiled=True)  14.1 us
    all_to_all x1, starting transfers between devices, body(): lax.all_to_all(up_z, 'gz', split_axis=1, concat_axis=0, tiled=True)  13.9 us
    all_to_all x1, waiting for transfers between devices, body(): lax.all_to_all(lines_x, 'gx', split_axis=1, concat_axis=0, tiled=True)  13.4 us
    ppermute x6, starting transfers between devices, extended(): after = lax.ppermute(leading, axis, down)  9.01 us
  transfers between devices with their start and end apart: 21, of which 14 were waited for; matrix products, arithmetic and copies ran while one was open for 45% of the time, Pallas kernels for 0%

commit v1 on v0

v1 whole, which is shorter than its diff:
```python
import functools

import jax
import jax.numpy as jnp
from jax import lax
from jax.experimental import pallas as pl
from jax.experimental.pallas import tpu as pltpu
from jax.sharding import PartitionSpec as P

MESH = pl.DeviceIdType.MESH
F32 = jnp.float32
RAW_TAPS = (0.41111229, 0.8007374, 1.0, 0.8007374, 0.41111229)
TAPS = tuple(tap / sum(RAW_TAPS) for tap in RAW_TAPS)
STIFFNESS = 9000.0
CONTRAST = 0.1
NEAR = tuple((dz, dy) for dz in (-1, 0, 1) for dy in (-1, 0, 1) if dz or dy)
SOLVERS = 4
FIRST_SOLVER = 2


def roll_z(tile, j):
    return pltpu.roll(tile, (-j) % 8, tile.ndim - 2)


def roll_y(tile, j):
    return pltpu.roll(tile, (-j) % 128, tile.ndim - 1)


def taps_sum(parts):
    return TAPS[2] * parts[2] + TAPS[1] * (parts[1] + parts[3]) + TAPS[0] * (parts[0] + parts[4])


def ring_z(tiles, t, j, row):
    if j == 0:
        return tiles[t]
    if j > 0:
        return jnp.where(row < 8 - j, roll_z(tiles[t], j), roll_z(tiles[1 - t], j))
    return jnp.where(row >= -j, roll_z(tiles[t], j), roll_z(tiles[1 - t], j))


def ring_y(tiles, t, j, lane):
    if j == 0:
        return tiles[t]
    if j > 0:
        return jnp.where(lane < 128 - j, roll_y(tiles[t], j), roll_y(tiles[(t + 1) % 3], j))
    return jnp.where(lane >= -j, roll_y(tiles[t], j), roll_y(tiles[(t + 2) % 3], j))


def wide_z(down, own, up, row):
    inner, outer = [], []
    for j in range(-2, 3):
        if j == 0:
            inner.append(own)
            outer.append(jnp.where(row < 4, up, down))
            continue
        down_j, own_j, up_j = roll_z(down, j), roll_z(own, j), roll_z(up, j)
        if j > 0:
            inner.append(jnp.where(row < 8 - j, own_j, up_j))
            outer.append(jnp.where(row < 4, up_j, jnp.where(row < 8 - j, down_j, own_j)))
        else:
            inner.append(jnp.where(row >= -j, own_j, down_j))
            outer.append(jnp.where(row >= 4, down_j, jnp.where(row >= -j, up_j, own_j)))
    return taps_sum(inner), taps_sum(outer)


def reduce_block(count, get_face, get_value, keep):
    series = get_face(0)
    left_ground = jnp.ones_like(series)
    left_source = get_value(0)
    ground = jnp.ones_like(series)
    source = get_value(1)
    for j in range(1, count):
        face = get_face(j)
        inverse = 1.0 / (series + ground + face)
        to_left, to_next = series * inverse, face * inverse
        keep(j, to_left, to_next, source * inverse)
        left_ground = left_ground + to_left * ground
        left_source = left_source + to_left * source
        series = to_left * face
        if j < count - 1:
            ground = 1.0 + to_next * ground
            source = get_value(j + 1) + to_next * source
    return series, left_ground, to_next * ground, left_source, to_next * source


def merge_blocks(left, right):
    a_l, gl_l, gr_l, il_l, ir_l = left
    a_r, gl_r, gr_r, il_r, ir_r = right
    ground, source = gr_l + gl_r, ir_l + il_r
    inverse = 1.0 / (a_l + ground + a_r)
    to_l, to_r = a_l * inverse, a_r * inverse
    merged = (to_l * a_r, gl_l + to_l * ground, gr_r + to_r * ground, il_l + to_l * source, ir_r + to_r * source)
    return merged, (to_l, to_r, source * inverse)


def ladder_rings(series, ground, source, count, axis):
    size = series.shape[axis]
    step = 1
    while step < count:
        def low(array):
            return pltpu.roll(array, step, axis)

        def high(array):
            return pltpu.roll(array, size - step, axis)

        before = low(series)
        inverse = 1.0 / (ground + series + before)
        from_low, from_high = before * low(inverse), series * high(inverse)
        ground, source, series = (
            ground + from_low * low(ground) + from_high * high(ground),
            source + from_low * low(source) + from_high * high(source),
            from_high * high(series),
        )
        step *= 2
    return source / ground


def kernel(v_ref, o_ref, B, C, BL, SQ, GX, GZ, GY, XA, XOWN, XPEER, XG, SG, ZA, PZ, ZPEER, MS, ZR, RT, RV, SEP,
           GT, VT, YA, PY, YG, YS, XY, GIVE, ss_h, rs_h, ss_x, rs_x, ss_p, rs_p, ss_c, rs_c, ss_y, rs_y, ss_k, rs_k,
           ss_a, rs_a, ss_r, rs_r, ss_b, rs_b):
    gx, gy, gz = lax.axis_index("gx"), lax.axis_index("gy"), lax.axis_index("gz")
    zc, core = lax.div(gz, 2), lax.rem(gz, 2)
    xc, zh = lax.div(gx, 2), lax.rem(gx, 2)
    other_core = gz + 1 - 2 * core
    row = lax.broadcasted_iota(jnp.int32, (8, 128), 0)
    lane = lax.broadcasted_iota(jnp.int32, (8, 128), 1)

    def inside(dz, dy):
        z, y = gz + dz, gy + dy
        return jnp.logical_and(jnp.logical_and(z >= 0, z < 16), jnp.logical_and(y >= 0, y < 4))

    barrier = pltpu.get_barrier_semaphore()
    always = []
    for d in (2, 4, 6):
        always.append({"gx": lax.rem(gx + d, 8)})
    for d in (1, 2, 3):
        always.append({"gy": lax.rem(gy + d, 4)})
    for d in range(1, 8):
        always.append({"gz": lax.rem(zc + d, 8) * 2 + core})
    total = jnp.int32(len(always))

    @pl.when(gx > 0)
    def _():
        pl.semaphore_signal(barrier, inc=1, device_id={"gx": gx - 1}, device_id_type=MESH)

    @pl.when(gx < 7)
    def _():
        pl.semaphore_signal(barrier, inc=1, device_id={"gx": gx + 1}, device_id_type=MESH)

    total = total + jnp.where(gx > 0, 1, 0) + jnp.where(gx < 7, 1, 0)
    for target in always:
        pl.semaphore_signal(barrier, inc=1, device_id=target, device_id_type=MESH)
    for dz, dy in NEAR:
        total = total + jnp.where(inside(dz, dy), 1, 0)

        @pl.when(inside(dz, dy))
        def _():
            pl.semaphore_signal(barrier, inc=1, device_id={"gz": gz + dz, "gy": gy + dy}, device_id_type=MESH)

    for yt in range(2):
        XY[yt] = v_ref[:, 128 * yt:128 * yt + 128]
    for x in range(16):
        for yt in range(2):
            B[1, 1 + yt, x] = XY[yt, pl.ds(x, 8, stride=16), :]

    @pl.when(gz == 0)
    def _():
        B[0] = jnp.zeros((4, 27, 8, 128), F32)

    @pl.when(gz == 15)
    def _():
        B[2] = jnp.zeros((4, 27, 8, 128), F32)

    @pl.when(gy == 0)
    def _():
        for zt in range(3):
            B[zt, 0] = jnp.zeros((27, 8, 128), F32)

    @pl.when(gy == 3)
    def _():
        for zt in range(3):
            B[zt, 3] = jnp.zeros((27, 8, 128), F32)

    @pl.when(gx == 0)
    def _():
        for yt in (1, 2):
            B[1, yt, 22:27] = jnp.zeros((5, 8, 128), F32)

    @pl.when(gx == 7)
    def _():
        for yt in (1, 2):
            B[1, yt, 16:22] = jnp.zeros((6, 8, 128), F32)

    pl.semaphore_wait(barrier, total)

    def x_copy(i):
        if i == 0:
            source, target, device = B.at[1, 1:3, 0:6], B.at[1, 1:3, 16:22], {"gx": gx - 1}
        else:
            source, target, device = B.at[1, 1:3, 11:16], B.at[1, 1:3, 22:27], {"gx": gx + 1}
        return pltpu.make_async_remote_copy(
            src_ref=source, dst_ref=target, send_sem=ss_x.at[i], recv_sem=rs_x.at[i],
            device_id=device, device_id_type=MESH)

    @pl.when(gx > 0)
    def _():
        x_copy(0).start()

    @pl.when(gx < 7)
    def _():
        x_copy(1).start()

    def near_copy(phase, i):
        dz, dy = NEAR[i]
        xs = slice(0, 16) if phase == 0 else slice(16, 27)
        ys, yd = {0: (slice(1, 3), slice(1, 3)), 1: (slice(2, 3), slice(0, 1)), -1: (slice(1, 2), slice(3, 4))}[dy]
        return pltpu.make_async_remote_copy(
            src_ref=B.at[1, ys, xs], dst_ref=B.at[1 - dz, yd, xs],
            send_sem=ss_h.at[phase, i], recv_sem=rs_h.at[phase, i],
            device_id={"gz": gz + dz, "gy": gy + dy}, device_id_type=MESH)

    def near_start(phase):
        for i, (dz, dy) in enumerate(NEAR):
            @pl.when(inside(dz, dy))
            def _():
                near_copy(phase, i).start()

    def near_recv(phase):
        for i, (dz, dy) in enumerate(NEAR):
            @pl.when(inside(-dz, -dy))
            def _():
                near_copy(phase, i).wait_recv()

    def near_send(phase):
        for i, (dz, dy) in enumerate(NEAR):
            @pl.when(inside(dz, dy))
            def _():
                near_copy(phase, i).wait_send()

    near_start(0)

    def blur_zy(xi):
        columns = []
        for zt in range(3):
            halo = jnp.where(lane < 64, B[zt, 3, xi], B[zt, 0, xi])
            columns.append([B[zt, 1, xi], B[zt, 2, xi], halo])
        inner, outer = [], []
        for yt in range(3):
            a, b = wide_z(columns[0][yt], columns[1][yt], columns[2][yt], row)
            inner.append(a)
            outer.append(b)
        place = lax.rem(xi + 5, 27)
        for zt, tiles in enumerate((inner, outer)):
            for yt in range(3):
                C[place, zt, yt] = taps_sum([ring_y(tiles, yt, j, lane) for j in range(-2, 3)])

    def blur_loop(first, last):
        def step(xi, carry):
            blur_zy(xi)
            return carry
        lax.fori_loop(first, last, step, 0)

    near_recv(0)
    blur_loop(0, 16)

    @pl.when(gx < 7)
    def _():
        x_copy(0).wait_recv()

    @pl.when(gx > 0)
    def _():
        x_copy(1).wait_recv()

    near_start(1)
    near_recv(1)
    blur_loop(16, 27)

    def blur_x(p, carry):
        for zt in range(2):
            for yt in range(3):
                BL[p, zt, yt] = taps_sum([C[p + j, zt, yt] for j in range(5)])
        return carry
    lax.fori_loop(0, 23, blur_x, 0)

    above = jnp.where(gz < 15, 0.5, 0.0)
    below = jnp.where(gz > 0, 0.5, 0.0)
    right = jnp.where(gy < 3, 1.0, 0.0)
    left = jnp.where(gy > 0, 1.0, 0.0)
    z_half = (jnp.full((8, 128), 0.5, F32), jnp.where(row < 4, above, below).astype(F32))
    y_one = jnp.where(lane < 64, right, left).astype(F32)
    halves = [[z_half[0], z_half[0], z_half[0] * y_one], [z_half[1], z_half[1], z_half[1] * y_one]]

    def slopes(p, carry):
        x_in = jnp.where(jnp.logical_or(jnp.logical_and(p < 2, gx == 0), jnp.logical_and(p > 17, gx == 7)), 0.0, 1.0)
        tiles = [[BL[p + 1, zt, yt] for yt in range(3)] for zt in range(2)]
        for zt in range(2):
            for yt in range(3):
                half = halves[zt][yt] * x_in
                slope_x = (BL[p + 2, zt, yt] - BL[p, zt, yt]) * half
                SQ[0, p, zt, yt] = slope_x * slope_x
                column = [tiles[0][yt], tiles[1][yt]]
                slope_z = (ring_z(column, zt, 1, row) - ring_z(column, zt, -1, row)) * half
                SQ[1, p, zt, yt] = slope_z * slope_z
                slope_y = (ring_y(tiles[zt], yt, 1, lane) - ring_y(tiles[zt], yt, -1, lane)) * half
                SQ[2, p, zt, yt] = slope_y * slope_y
        return carry
    lax.fori_loop(0, 21, slopes, 0)

    def diffuse(tensor):
        return 1.0 / (1.0 + tensor * (1.0 / (CONTRAST * CONTRAST)))

    def tensor_x(a, p):
        return [[taps_sum([SQ[a, p + j, zt, yt] for j in range(5)]) for yt in range(3)] for zt in range(2)]

    def tensor_z(tiles, zt):
        return [taps_sum([ring_z([tiles[0][yt], tiles[1][yt]], zt, j, row) for j in range(-2, 3)]) for yt in range(3)]

    def tensor_y(tiles, yt):
        return taps_sum([ring_y(tiles, yt, j, lane) for j in range(-2, 3)])

    def face_x(p, before):
        tiles = tensor_z(tensor_x(0, p), 0)
        now = jnp.stack([diffuse(tensor_y(tiles, yt)) for yt in range(2)])
        scale = jnp.where(jnp.logical_and(p == 16, gx == 7), 0.0, 0.5 * STIFFNESS)

        @pl.when(p > 0)
        def _():
            GX[jnp.maximum(p - 1, 0)] = (before + now) * scale
        return now
    lax.fori_loop(0, 17, face_x, jnp.zeros((2, 8, 128), F32))

    def keep_x(j, to_left, to_next, source):
        XA[0, j], XA[1, j], XA[2, j] = to_left, to_next, source

    own_x = reduce_block(16, lambda j: GX[j], lambda j: B[1, 1:3, j], keep_x)
    for i in range(5):
        XOWN[i] = own_x[i]
    pair = pltpu.make_async_remote_copy(
        src_ref=XOWN, dst_ref=XPEER, send_sem=ss_p, recv_sem=rs_p,
        device_id={"gx": gx + 1 - 2 * zh}, device_id_type=MESH)
    pair.start()

    z_scale = jnp.where(jnp.logical_and(row == 7, gz == 15), 0.0, 0.5 * STIFFNESS).astype(F32)

    def face_z(p, carry):
        tiles = tensor_x(1, p)
        rows = [tensor_z(tiles, zt) for zt in range(2)]
        at = pl.multiple_of(p * 8, 8)
        for yt in range(2):
            own, halo = diffuse(tensor_y(rows[0], yt)), diffuse(tensor_y(rows[1], yt))
            GZ[yt, pl.ds(at, 8), :] = (own + ring_z([own, halo], 0, 1, row)) * z_scale
        return carry
    lax.fori_loop(0, 16, face_z, 0)

    def keep_z(j, to_left, to_next, source):
        ZA[0, j], ZA[1, j], ZA[2, j] = to_left, to_next, source

    def get_gz(j):
        return jnp.stack([GZ[yt, pl.ds(j, 16, stride=8), :] for yt in range(2)])

    def get_vz(j):
        return jnp.stack([v_ref[16 * j:16 * j + 16, 128 * yt:128 * yt + 128] for yt in range(2)])

    own_z = reduce_block(8, get_gz, get_vz, keep_z)
    for i in range(5):
        for h in range(2):
            PZ[h, i] = own_z[i][:, 8 * h:8 * h + 8, :]
    cores = pltpu.make_async_remote_copy(
        src_ref=PZ.at[1 - core], dst_ref=ZPEER, send_sem=ss_k, recv_sem=rs_k,
        device_id={"gz": other_core}, device_id_type=MESH)
    cores.start()

    y_scale = (jnp.full((8, 128), 0.5 * STIFFNESS, F32),
               jnp.where(jnp.logical_and(lane == 127, gy == 3), 0.0, 0.5 * STIFFNESS).astype(F32))

    def face_y(p, carry):
        tiles = tensor_z(tensor_x(2, p), 0)
        values = [diffuse(tensor_y(tiles, yt)) for yt in range(3)]
        at = pl.multiple_of(p * 8, 8)
        for yt in range(2):
            GY[yt, pl.ds(at, 8), :] = (values[yt] + ring_y(values, yt, 1, lane)) * y_scale[yt]
        return carry
    lax.fori_loop(0, 16, face_y, 0)

    cores.wait_recv()
    mine = [PZ[core, i] for i in range(5)]
    peer = [ZPEER[i] for i in range(5)]
    low = core == 0
    merged_z, middle_z = merge_blocks([jnp.where(low, a, b) for a, b in zip(mine, peer)],
                                      [jnp.where(low, b, a) for a, b in zip(mine, peer)])
    for i in range(5):
        for yt in range(2):
            MS[pl.ds(2 * i + yt, 8, stride=16), :] = merged_z[i][yt]

    def to_solver(k):
        return pltpu.make_async_remote_copy(
            src_ref=MS.at[pl.ds(32 * k, 32)], dst_ref=ZR.at[pl.ds(pl.multiple_of(zc * 32, 32), 32)],
            send_sem=ss_a.at[k], recv_sem=rs_a.at[zc],
            device_id={"gz": 2 * (FIRST_SOLVER + k) + core}, device_id_type=MESH)

    def from_chip(p):
        return pltpu.make_async_remote_copy(
            src_ref=MS.at[pl.ds(0, 32)], dst_ref=ZR.at[pl.ds(32 * p, 32)],
            send_sem=ss_a.at[0], recv_sem=rs_a.at[p],
            device_id={"gz": other_core}, device_id_type=MESH)

    for k in range(SOLVERS):
        @pl.when(zc != FIRST_SOLVER + k)
        def _():
            to_solver(k).start()

        @pl.when(zc == FIRST_SOLVER + k)
        def _():
            ZR[32 * (FIRST_SOLVER + k):32 * (FIRST_SOLVER + k) + 32, :] = MS[32 * k:32 * k + 32, :]

    for yt in range(2):
        GT[128 * yt:128 * yt + 128, :] = GY[yt].T
        VT[128 * yt:128 * yt + 128, :] = B[1, 1 + yt, 0:16].reshape(128, 128).T

    def keep_y(j, to_left, to_next, source):
        YA[0, j], YA[1, j], YA[2, j] = to_left, to_next, source

    own_y = reduce_block(32, lambda j: GT[pl.ds(j, 8, stride=32), :], lambda j: VT[pl.ds(j, 8, stride=32), :], keep_y)
    for i in range(5):
        PY[i] = own_y[i]

    def y_copy(d):
        return pltpu.make_async_remote_copy(
            src_ref=PY, dst_ref=YG.at[gy], send_sem=ss_y.at[d - 1], recv_sem=rs_y.at[d - 1],
            device_id={"gy": lax.rem(gy + d, 4)}, device_id_type=MESH)

    def y_back(d):
        return pltpu.make_async_remote_copy(
            src_ref=PY, dst_ref=YG.at[lax.rem(gy + 4 - d, 4)], send_sem=ss_y.at[d - 1], recv_sem=rs_y.at[d - 1],
            device_id={"gy": lax.rem(gy + d, 4)}, device_id_type=MESH)

    for d in (1, 2, 3):
        y_copy(d).start()
    YG[gy] = PY[...]

    is_solver = jnp.logical_and(zc >= FIRST_SOLVER, zc < FIRST_SOLVER + SOLVERS)
    place = jnp.clip(zc - FIRST_SOLVER, 0, SOLVERS - 1)

    def to_chip(p):
        return pltpu.make_async_remote_copy(
            src_ref=RT.at[pl.ds(8 * p, 8)], dst_ref=RV.at[pl.ds(pl.multiple_of(place * 8, 8), 8)],
            send_sem=ss_r.at[p], recv_sem=rs_r.at[place],
            device_id={"gz": 2 * p + core}, device_id_type=MESH)

    def from_solver(k):
        return pltpu.make_async_remote_copy(
            src_ref=RT.at[pl.ds(0, 8)], dst_ref=RV.at[pl.ds(8 * k, 8)],
            send_sem=ss_r.at[0], recv_sem=rs_r.at[k],
            device_id={"gz": other_core}, device_id_type=MESH)

    @pl.when(is_solver)
    def _():
        for p in range(8):
            @pl.when(zc != p)
            def _():
                from_chip(p).wait_recv()

        def gather(i):
            return jnp.stack([ZR[pl.ds(16 * rr + 2 * i + yt, 8, stride=32), :] for rr in range(2) for yt in range(2)])
        series, gl, gr, il, ir = [gather(i) for i in range(5)]
        sigma = ladder_rings(series, gl + pltpu.roll(gr, 1, 1), il + pltpu.roll(ir, 1, 1), 8, 1)
        following = pltpu.roll(sigma, 7, 1)
        for rr in range(2):
            for yt in range(2):
                RT[pl.ds(4 * rr + yt, 8, stride=8), :] = sigma[2 * rr + yt]
                RT[pl.ds(4 * rr + 2 + yt, 8, stride=8), :] = following[2 * rr + yt]
        for p in range(8):
            @pl.when(zc != p)
            def _():
                to_chip(p).start()

            @pl.when(zc == p)
            def _():
                RV[pl.ds(pl.multiple_of(place * 8, 8), 8), :] = RT[8 * p:8 * p + 8, :]

    for d in (1, 2, 3):
        y_back(d).wait_recv()
    series, gl, gr, il, ir = [YG[:, i].reshape(32, 128) for i in range(5)]
    sigma = ladder_rings(series, gl + pltpu.roll(gr, 1, 0), il + pltpu.roll(ir, 1, 0), 32, 0)
    YS[0] = sigma.reshape(4, 8, 128)
    YS[1] = pltpu.roll(sigma, 31, 0).reshape(4, 8, 128)
    first, solved = YS[0, gy], YS[1, gy]
    VT[pl.ds(0, 8, stride=32), :] = first
    for j in range(31, 0, -1):
        solved = YA[2, j] + YA[0, j] * first + YA[1, j] * solved
        VT[pl.ds(j, 8, stride=32), :] = solved
    for yt in range(2):
        XY[yt] = VT[128 * yt:128 * yt + 128, :].T

    pair.wait_recv()
    mine = [XOWN[i] for i in range(5)]
    peer = [XPEER[i] for i in range(5)]
    low_x = zh == 0
    merged_x, middle_x = merge_blocks([jnp.where(low_x, a, b) for a, b in zip(mine, peer)],
                                      [jnp.where(low_x, b, a) for a, b in zip(mine, peer)])
    for i in range(5):
        XG[xc, i] = merged_x[i]

    def xg_copy(d):
        return pltpu.make_async_remote_copy(
            src_ref=XG.at[xc], dst_ref=XG.at[xc], send_sem=ss_c.at[d - 1], recv_sem=rs_c.at[d - 1],
            device_id={"gx": lax.rem(gx + 2 * d, 8)}, device_id_type=MESH)

    def xg_back(d):
        return pltpu.make_async_remote_copy(
            src_ref=XG.at[xc], dst_ref=XG.at[lax.rem(xc + 4 - d, 4)], send_sem=ss_c.at[d - 1], recv_sem=rs_c.at[d - 1],
            device_id={"gx": lax.rem(gx + 2 * d, 8)}, device_id_type=MESH)

    for d in (1, 2, 3):
        xg_copy(d).start()

    for k in range(SOLVERS):
        @pl.when(zc != FIRST_SOLVER + k)
        def _():
            from_solver(k).wait_recv()

    def ends(w):
        return jnp.stack([RV[pl.ds(2 * w + yt, 8, stride=4), :] for yt in range(2)])
    start, end = ends(0), ends(1)
    middle = middle_z[2] + middle_z[0] * start + middle_z[1] * end
    SEP[core, 0] = jnp.where(low, start, middle)
    SEP[core, 1] = jnp.where(low, middle, end)
    GIVE[0] = jnp.where(low, middle, start)
    GIVE[1] = jnp.where(low, end, middle)
    give = pltpu.make_async_remote_copy(
        src_ref=GIVE, dst_ref=SEP.at[core], send_sem=ss_b, recv_sem=rs_b,
        device_id={"gz": other_core}, device_id_type=MESH)
    give.start()

    for d in (1, 2, 3):
        xg_back(d).wait_recv()
    ground, source = XG[0, 1], XG[0, 3]
    stack = []
    for p in range(4):
        series = XG[p, 0]
        inverse = 1.0 / (ground + series)
        ratio = series * inverse
        stack.append((source * inverse, ratio))
        if p < 3:
            ground = XG[p + 1, 1] + XG[p, 2] + ratio * ground
            source = XG[p + 1, 3] + XG[p, 4] + ratio * source
    value = stack[3][0]
    SG[4] = jnp.zeros((2, 8, 128), F32)
    SG[3] = value
    for p in (2, 1, 0):
        value = stack[p][0] + stack[p][1] * value
        SG[p] = value
    start_x, end_x = SG[xc], SG[xc + 1]
    middle_node = middle_x[2] + middle_x[0] * start_x + middle_x[1] * end_x
    first = jnp.where(low_x, start_x, middle_node)
    solved = jnp.where(low_x, middle_node, end_x)

    def add_x(j, value):
        for yt in range(2):
            XY[yt, 8 * j:8 * j + 8, :] = XY[yt, 8 * j:8 * j + 8, :] + value[yt]
    add_x(0, first)
    for j in range(15, 0, -1):
        solved = XA[2, j] + XA[0, j] * first + XA[1, j] * solved
        add_x(j, solved)

    pltpu.make_async_remote_copy(
        src_ref=GIVE, dst_ref=SEP.at[1 - core], send_sem=ss_b, recv_sem=rs_b,
        device_id={"gz": other_core}, device_id_type=MESH).wait_recv()
    first = jnp.concatenate([SEP[0, 0], SEP[1, 0]], axis=1)
    solved = jnp.concatenate([SEP[0, 1], SEP[1, 1]], axis=1)

    def write(j, value):
        for yt in range(2):
            o_ref[16 * j:16 * j + 16, 128 * yt:128 * yt + 128] = value[yt] + XY[yt, pl.ds(j, 16, stride=8), :]
    write(0, first)
    for j in range(7, 0, -1):
        solved = ZA[2, j] + ZA[0, j] * first + ZA[1, j] * solved
        write(j, solved)

    @pl.when(gx > 0)
    def _():
        x_copy(0).wait_send()

    @pl.when(gx < 7)
    def _():
        x_copy(1).wait_send()
    near_send(0)
    near_send(1)
    pair.wait_send()
    for d in (1, 2, 3):
        y_copy(d).wait_send()
        xg_copy(d).wait_send()
    for k in range(SOLVERS):
        @pl.when(zc != FIRST_SOLVER + k)
        def _():
            to_solver(k).wait_send()

    @pl.when(is_solver)
    def _():
        for p in range(8):
            @pl.when(zc != p)
            def _():
                to_chip(p).wait_send()
    cores.wait_send()
    give.wait_send()


def body(volume):
    tile = (8, 128)
    dma = pltpu.SemaphoreType.DMA
    vmem = [
        (3, 4, 27) + tile,
        (27, 2, 3) + tile,
        (23, 2, 3) + tile,
        (3, 21, 2, 3) + tile,
        (16, 2) + tile,
        (2, 128, 128),
        (2, 128, 128),
        (3, 16, 2) + tile,
        (5, 2) + tile,
        (5, 2) + tile,
        (4, 5, 2) + tile,
        (5, 2) + tile,
        (3, 8, 2, 16, 128),
        (2, 5, 2) + tile,
        (5, 2) + tile,
        (128, 128),
        (256, 128),
        (64, 128),
        (32, 128),
        (2, 2, 2) + tile,
        (256, 128),
        (256, 128),
        (3, 32) + tile,
        (5,) + tile,
        (4, 5) + tile,
        (2, 4) + tile,
        (2, 128, 128),
        (2, 2) + tile,
    ]
    sems = [(2, 8), (2, 8), (2,), (2,), None, None, (3,), (3,), (3,), (3,), None, None, (4,), (8,), (8,), (4,), None, None]
    total = pl.pallas_call(
        kernel,
        out_shape=jax.ShapeDtypeStruct((128, 256), F32),
        in_specs=[pl.BlockSpec(memory_space=pltpu.VMEM)],
        out_specs=pl.BlockSpec(memory_space=pltpu.VMEM),
        scratch_shapes=[pltpu.VMEM(shape, F32) for shape in vmem] + [dma(s) if s else dma for s in sems],
        compiler_params=pltpu.CompilerParams(
            collective_id=0, has_side_effects=True, vmem_limit_bytes=24 * 2**20),
        cost_estimate=pl.CostEstimate(flops=40_000_000, bytes_accessed=262144, transcendentals=0),
    )(volume.reshape(128, 256))
    return (total / 3.0).reshape(8, 16, 256)


def solution(mesh):
    return jax.shard_map(
        body,
        mesh=mesh,
        in_specs=(P("gz", "gx", "gy"),),
        out_specs=P("gz", "gx", "gy"),
        check_vma=False,
    )
```

time: 382 us -> 58.9 us (0.15)
  the two profiles are of different devices: /device:TPU:1 before, /device:TPU:19 now
where the time goes in v1:
time: 58.9 us; the launch traced here: 58.8 us
  Pallas kernels  57.2 us (97%)
  local copies, waits for them, and re-layouts  0.9 us (2%)
  other arithmetic  0.67 us (1%)
    pallas_call x1, Pallas kernels, body(): pl.pallas_call(kernel, out_shape=jax.ShapeDtypeStruct((128, 256), F32), i...  57.2 us

profile of v1, /device:TPU:19, one launch (start us, length us, event | category | flops | bytes accessed | tf_op | source)
XLA Modules:
  0.0 58.8 jit_solution(4904977936615286075)
XLA Ops:
  0.0 0.0 copy-start
  0.0 0.9 %copy-done = f32[8,16,256]{2,1,0:T(8,128)S(1)} copy-done((f32[8,16,256]{2,1,0:T(8,128)S(1)}, f32[8,16,256]{2,1,0:T(8,128)}, u32[]{:S(2)}) %copy-start) | copy-done | bytes 131096
  0.9 57.2 %shard_map.17 = f32[128,256]{1,0:T(8,128)S(1)} custom-call(f32[128,256]{1,0:T(8,128)S(1)} %bitcast.2), custom_call_target="tpu_custom_call" | custom-call | flops 40000000 | bytes 262144 | tf_op jit(solution)/shard_map/pallas_call | solution.py:642
  58.1 0.7 %broadcast_multiply_fusion = f32[128,256]{1,0:T(8,128)} fusion(f32[128,256]{1,0:T(8,128)S(1)} %shard_map.17), kind=kLoop, calls=%fused_computation | loop fusion | flops 32768 | bytes 262144 | tf_op jit(solution)/shard_map/div | solution.py:652
Async XLA Ops:
  0.0 0.9 %copy-start = (f32[8,16,256]{2,1,0:T(8,128)S(1)}, f32[8,16,256]{2,1,0:T(8,128)}, u32[]{:S(2)}) copy-start(f32[8,16,256]{2,1,0:T(8,128)} %param.1) | copy-start | bytes 393220

commit v2 on v1

--- a/solution.py
+++ b/solution.py
@@ -16,6 +16,7 @@
 NEAR = tuple((dz, dy) for dz in (-1, 0, 1) for dy in (-1, 0, 1) if dz or dy)
 SOLVERS = 4
 FIRST_SOLVER = 2
+U_BLUR, U_X, U_SLOPE, U_FACE = 2, 2, 2, 2
 
 
 def roll_z(tile, j):
@@ -61,6 +62,19 @@
             inner.append(jnp.where(row >= -j, own_j, down_j))
             outer.append(jnp.where(row >= 4, down_j, jnp.where(row >= -j, up_j, own_j)))
     return taps_sum(inner), taps_sum(outer)
+
+
+def loop(first, last, step, unroll):
+    trips = (last - first) // unroll
+
+    def some(t, carry):
+        for u in range(unroll):
+            step(first + t * unroll + u)
+        return carry
+    if trips:
+        lax.fori_loop(0, trips, some, 0)
+    for i in range(first + trips * unroll, last):
+        step(i)
 
 
 def reduce_block(count, get_face, get_value, keep):
@@ -115,13 +129,19 @@
     return source / ground
 
 
-def kernel(v_ref, o_ref, B, C, BL, SQ, GX, GZ, GY, XA, XOWN, XPEER, XG, SG, ZA, PZ, ZPEER, MS, ZR, RT, RV, SEP,
-           GT, VT, YA, PY, YG, YS, XY, GIVE, ss_h, rs_h, ss_x, rs_x, ss_p, rs_p, ss_c, rs_c, ss_y, rs_y, ss_k, rs_k,
-           ss_a, rs_a, ss_r, rs_r, ss_b, rs_b):
+def kernel(v_hbm, o_ref, v_ref, B, HS, HB, RB0, RB1, C, BL, SQ, GZ, GY, XA, XOWN, XPEER, XG, SG, ZA, PZ, ZPEER,
+           MS, ZR, RT, RV, SEP, GT, VT, YA, PY, YG, YS, XY, GIVE, in_sem, ss_h, rs_h, ss_x, rs_x, ss_f, rs_f, ss_p, rs_p,
+           ss_c, rs_c, ss_y, rs_y, ss_k, rs_k, ss_a, rs_a, ss_r, rs_r, ss_b, rs_b):
     gx, gy, gz = lax.axis_index("gx"), lax.axis_index("gy"), lax.axis_index("gz")
     zc, core = lax.div(gz, 2), lax.rem(gz, 2)
     xc, zh = lax.div(gx, 2), lax.rem(gx, 2)
     other_core = gz + 1 - 2 * core
+    load = pltpu.make_async_copy(v_hbm, v_ref, in_sem)
+    load.start()
+
+    def chip_at(from_gx, dz):
+        z = lax.rem(lax.rem(from_gx, 2) * 8 + zc + 16 + dz, 16)
+        return lax.div(from_gx, 2) * 2 + lax.div(z, 8), lax.rem(z, 8) * 2 + core
     row = lax.broadcasted_iota(jnp.int32, (8, 128), 0)
     lane = lax.broadcasted_iota(jnp.int32, (8, 128), 1)
 
@@ -130,26 +150,37 @@
         return jnp.logical_and(jnp.logical_and(z >= 0, z < 16), jnp.logical_and(y >= 0, y < 4))
 
     barrier = pltpu.get_barrier_semaphore()
-    always = []
+    above_gx, above_gz = chip_at(gx, 4)
+    below_gx, below_gz = chip_at(gx, -4)
+    via_high = chip_at(gx + 1, 4)
+    via_low = chip_at(jnp.maximum(gx - 1, 0), -4)
+    always = [{"gx": above_gx, "gz": above_gz}, {"gx": below_gx, "gz": below_gz}]
     for d in (2, 4, 6):
         always.append({"gx": lax.rem(gx + d, 8)})
     for d in (1, 2, 3):
         always.append({"gy": lax.rem(gy + d, 4)})
-    for d in range(1, 8):
-        always.append({"gz": lax.rem(zc + d, 8) * 2 + core})
+    is_solver = jnp.logical_and(zc >= FIRST_SOLVER, zc < FIRST_SOLVER + SOLVERS)
     total = jnp.int32(len(always))
 
+    @pl.when(gx < 7)
+    def _():
+        pl.semaphore_signal(barrier, inc=1, device_id={"gx": via_high[0], "gz": via_high[1]}, device_id_type=MESH)
+
     @pl.when(gx > 0)
     def _():
-        pl.semaphore_signal(barrier, inc=1, device_id={"gx": gx - 1}, device_id_type=MESH)
-
-    @pl.when(gx < 7)
-    def _():
-        pl.semaphore_signal(barrier, inc=1, device_id={"gx": gx + 1}, device_id_type=MESH)
-
-    total = total + jnp.where(gx > 0, 1, 0) + jnp.where(gx < 7, 1, 0)
+        pl.semaphore_signal(barrier, inc=1, device_id={"gx": via_low[0], "gz": via_low[1]}, device_id_type=MESH)
+
+    total = total + jnp.where(below_gx > 0, 1, 0) + jnp.where(above_gx < 7, 1, 0)
     for target in always:
         pl.semaphore_signal(barrier, inc=1, device_id=target, device_id_type=MESH)
+    for p in range(8):
+        solves = FIRST_SOLVER <= p < FIRST_SOLVER + SOLVERS
+        meets = zc != p if solves else is_solver
+        total = total + jnp.where(meets, 1, 0)
+
+        @pl.when(meets)
+        def _():
+            pl.semaphore_signal(barrier, inc=1, device_id={"gz": 2 * p + core}, device_id_type=MESH)
     for dz, dy in NEAR:
         total = total + jnp.where(inside(dz, dy), 1, 0)
 
@@ -157,93 +188,126 @@
         def _():
             pl.semaphore_signal(barrier, inc=1, device_id={"gz": gz + dz, "gy": gy + dy}, device_id_type=MESH)
 
+    def pack(phase, layers):
+        low, high = None, None
+        for i, x in enumerate(layers):
+            a, b = B[1, 0, x], B[1, 1, x]
+            a = pltpu.roll(a, 8 * i, 1) if i else a
+            b = pltpu.roll(b, (8 * i + 8) % 128, 1) if i < 15 else b
+            low = a if low is None else jnp.where(lane < 8 * i, low, a)
+            high = b if high is None else jnp.where(lane < 8 * i, high, b)
+        HS[0, phase], HS[1, phase] = low, high
+
+    load.wait()
     for yt in range(2):
         XY[yt] = v_ref[:, 128 * yt:128 * yt + 128]
     for x in range(16):
         for yt in range(2):
-            B[1, 1 + yt, x] = XY[yt, pl.ds(x, 8, stride=16), :]
+            B[1, yt, x] = XY[yt, pl.ds(x, 8, stride=16), :]
+    pack(0, range(16))
 
     @pl.when(gz == 0)
     def _():
-        B[0] = jnp.zeros((4, 27, 8, 128), F32)
+        B[0] = jnp.zeros((2, 27, 8, 128), F32)
+        HB[0] = jnp.zeros((2, 2, 8, 128), F32)
 
     @pl.when(gz == 15)
     def _():
-        B[2] = jnp.zeros((4, 27, 8, 128), F32)
+        B[2] = jnp.zeros((2, 27, 8, 128), F32)
+        HB[2] = jnp.zeros((2, 2, 8, 128), F32)
 
     @pl.when(gy == 0)
     def _():
         for zt in range(3):
-            B[zt, 0] = jnp.zeros((27, 8, 128), F32)
+            HB[zt, 0] = jnp.zeros((2, 8, 128), F32)
 
     @pl.when(gy == 3)
     def _():
         for zt in range(3):
-            B[zt, 3] = jnp.zeros((27, 8, 128), F32)
+            HB[zt, 1] = jnp.zeros((2, 8, 128), F32)
 
     @pl.when(gx == 0)
     def _():
-        for yt in (1, 2):
+        for yt in range(2):
             B[1, yt, 22:27] = jnp.zeros((5, 8, 128), F32)
 
     @pl.when(gx == 7)
     def _():
-        for yt in (1, 2):
+        for yt in range(2):
             B[1, yt, 16:22] = jnp.zeros((6, 8, 128), F32)
 
     pl.semaphore_wait(barrier, total)
 
-    def x_copy(i):
-        if i == 0:
-            source, target, device = B.at[1, 1:3, 0:6], B.at[1, 1:3, 16:22], {"gx": gx - 1}
-        else:
-            source, target, device = B.at[1, 1:3, 11:16], B.at[1, 1:3, 22:27], {"gx": gx + 1}
-        return pltpu.make_async_remote_copy(
-            src_ref=source, dst_ref=target, send_sem=ss_x.at[i], recv_sem=rs_x.at[i],
+    def x_first(i, yt):
+        source, relay, device = ((B.at[1, yt, 0:6], RB0, {"gx": above_gx, "gz": above_gz}),
+                                 (B.at[1, yt, 11:16], RB1, {"gx": below_gx, "gz": below_gz}))[i]
+        return pltpu.make_async_remote_copy(
+            src_ref=source, dst_ref=relay.at[yt], send_sem=ss_f.at[i, yt], recv_sem=rs_f.at[i, yt],
             device_id=device, device_id_type=MESH)
 
-    @pl.when(gx > 0)
-    def _():
-        x_copy(0).start()
-
-    @pl.when(gx < 7)
-    def _():
-        x_copy(1).start()
-
-    def near_copy(phase, i):
+    def x_second(i, yt):
+        relay, target, device = ((RB0, B.at[1, yt, 16:22], {"gx": below_gx - 1, "gz": below_gz}),
+                                 (RB1, B.at[1, yt, 22:27], {"gx": above_gx + 1, "gz": above_gz}))[i]
+        return pltpu.make_async_remote_copy(
+            src_ref=relay.at[yt], dst_ref=target, send_sem=ss_x.at[i, yt], recv_sem=rs_x.at[i, yt],
+            device_id=device, device_id_type=MESH)
+
+    sends_x = (gx > 0, gx < 7)
+    relays_x = (below_gx > 0, above_gx < 7)
+    gets_x = (gx < 7, gx > 0)
+    both = [(i, yt) for yt in range(2) for i in range(2)]
+
+    for i, yt in both:
+        @pl.when(sends_x[i])
+        def _():
+            x_first(i, yt).start()
+
+    def near_copies(phase, i):
         dz, dy = NEAR[i]
         xs = slice(0, 16) if phase == 0 else slice(16, 27)
-        ys, yd = {0: (slice(1, 3), slice(1, 3)), 1: (slice(2, 3), slice(0, 1)), -1: (slice(1, 2), slice(3, 4))}[dy]
-        return pltpu.make_async_remote_copy(
-            src_ref=B.at[1, ys, xs], dst_ref=B.at[1 - dz, yd, xs],
-            send_sem=ss_h.at[phase, i], recv_sem=rs_h.at[phase, i],
+        if dy == 0:
+            source, target = B.at[1, :, xs], B.at[1 - dz, :, xs]
+        elif dy == 1:
+            source, target = HS.at[1, phase], HB.at[1 - dz, 0, phase]
+        else:
+            source, target = HS.at[0, phase], HB.at[1 - dz, 1, phase]
+        return pltpu.make_async_remote_copy(
+            src_ref=source, dst_ref=target, send_sem=ss_h.at[phase, i], recv_sem=rs_h.at[phase, i],
             device_id={"gz": gz + dz, "gy": gy + dy}, device_id_type=MESH)
 
     def near_start(phase):
         for i, (dz, dy) in enumerate(NEAR):
             @pl.when(inside(dz, dy))
             def _():
-                near_copy(phase, i).start()
+                near_copies(phase, i).start()
 
     def near_recv(phase):
         for i, (dz, dy) in enumerate(NEAR):
             @pl.when(inside(-dz, -dy))
             def _():
-                near_copy(phase, i).wait_recv()
+                near_copies(phase, i).wait_recv()
 
     def near_send(phase):
         for i, (dz, dy) in enumerate(NEAR):
             @pl.when(inside(dz, dy))
             def _():
-                near_copy(phase, i).wait_send()
+                near_copies(phase, i).wait_send()
 
     near_start(0)
 
-    def blur_zy(xi):
+    for i, yt in both:
+        @pl.when(relays_x[i])
+        def _():
+            x_first(i, yt).wait_recv()
+            x_second(i, yt).start()
+
+    def blur_zy(xi, phase):
         columns = []
+        layer = xi - 16 * phase
+        to_low, to_high = lax.rem(128 - 8 * layer, 128), 120 - 8 * layer
         for zt in range(3):
-            halo = jnp.where(lane < 64, B[zt, 3, xi], B[zt, 0, xi])
-            columns.append([B[zt, 1, xi], B[zt, 2, xi], halo])
+            halo = jnp.where(lane < 64, pltpu.roll(HB[zt, 1, phase], to_low, 1), pltpu.roll(HB[zt, 0, phase], to_high, 1))
+            columns.append([B[zt, 0, xi], B[zt, 1, xi], halo])
         inner, outer = [], []
         for yt in range(3):
             a, b = wide_z(columns[0][yt], columns[1][yt], columns[2][yt], row)
@@ -254,33 +318,10 @@
             for yt in range(3):
                 C[place, zt, yt] = taps_sum([ring_y(tiles, yt, j, lane) for j in range(-2, 3)])
 
-    def blur_loop(first, last):
-        def step(xi, carry):
-            blur_zy(xi)
-            return carry
-        lax.fori_loop(first, last, step, 0)
-
-    near_recv(0)
-    blur_loop(0, 16)
-
-    @pl.when(gx < 7)
-    def _():
-        x_copy(0).wait_recv()
-
-    @pl.when(gx > 0)
-    def _():
-        x_copy(1).wait_recv()
-
-    near_start(1)
-    near_recv(1)
-    blur_loop(16, 27)
-
-    def blur_x(p, carry):
+    def blur_x(p):
         for zt in range(2):
             for yt in range(3):
                 BL[p, zt, yt] = taps_sum([C[p + j, zt, yt] for j in range(5)])
-        return carry
-    lax.fori_loop(0, 23, blur_x, 0)
 
     above = jnp.where(gz < 15, 0.5, 0.0)
     below = jnp.where(gz > 0, 0.5, 0.0)
@@ -290,7 +331,7 @@
     y_one = jnp.where(lane < 64, right, left).astype(F32)
     halves = [[z_half[0], z_half[0], z_half[0] * y_one], [z_half[1], z_half[1], z_half[1] * y_one]]
 
-    def slopes(p, carry):
+    def slopes(p):
         x_in = jnp.where(jnp.logical_or(jnp.logical_and(p < 2, gx == 0), jnp.logical_and(p > 17, gx == 7)), 0.0, 1.0)
         tiles = [[BL[p + 1, zt, yt] for yt in range(3)] for zt in range(2)]
         for zt in range(2):
@@ -303,8 +344,25 @@
                 SQ[1, p, zt, yt] = slope_z * slope_z
                 slope_y = (ring_y(tiles[zt], yt, 1, lane) - ring_y(tiles[zt], yt, -1, lane)) * half
                 SQ[2, p, zt, yt] = slope_y * slope_y
-        return carry
-    lax.fori_loop(0, 21, slopes, 0)
+
+    near_recv(0)
+    loop(0, 16, lambda xi: blur_zy(xi, 0), U_BLUR)
+    loop(5, 17, blur_x, U_X)
+    loop(5, 15, slopes, U_SLOPE)
+
+    for i, yt in both:
+        @pl.when(gets_x[i])
+        def _():
+            x_second(i, yt).wait_recv()
+
+    pack(1, range(16, 27))
+    near_start(1)
+    near_recv(1)
+    loop(16, 27, lambda xi: blur_zy(xi, 1), U_BLUR)
+    loop(0, 5, blur_x, U_X)
+    loop(17, 23, blur_x, U_X)
+    loop(0, 5, slopes, U_SLOPE)
+    loop(15, 21, slopes, U_SLOPE)
 
     def diffuse(tensor):
         return 1.0 / (1.0 + tensor * (1.0 / (CONTRAST * CONTRAST)))
@@ -318,39 +376,16 @@
     def tensor_y(tiles, yt):
         return taps_sum([ring_y(tiles, yt, j, lane) for j in range(-2, 3)])
 
-    def face_x(p, before):
-        tiles = tensor_z(tensor_x(0, p), 0)
-        now = jnp.stack([diffuse(tensor_y(tiles, yt)) for yt in range(2)])
-        scale = jnp.where(jnp.logical_and(p == 16, gx == 7), 0.0, 0.5 * STIFFNESS)
-
-        @pl.when(p > 0)
-        def _():
-            GX[jnp.maximum(p - 1, 0)] = (before + now) * scale
-        return now
-    lax.fori_loop(0, 17, face_x, jnp.zeros((2, 8, 128), F32))
-
-    def keep_x(j, to_left, to_next, source):
-        XA[0, j], XA[1, j], XA[2, j] = to_left, to_next, source
-
-    own_x = reduce_block(16, lambda j: GX[j], lambda j: B[1, 1:3, j], keep_x)
-    for i in range(5):
-        XOWN[i] = own_x[i]
-    pair = pltpu.make_async_remote_copy(
-        src_ref=XOWN, dst_ref=XPEER, send_sem=ss_p, recv_sem=rs_p,
-        device_id={"gx": gx + 1 - 2 * zh}, device_id_type=MESH)
-    pair.start()
-
     z_scale = jnp.where(jnp.logical_and(row == 7, gz == 15), 0.0, 0.5 * STIFFNESS).astype(F32)
 
-    def face_z(p, carry):
+    def face_z(p):
         tiles = tensor_x(1, p)
         rows = [tensor_z(tiles, zt) for zt in range(2)]
-        at = pl.multiple_of(p * 8, 8)
+        at = p * 8 if isinstance(p, int) else pl.multiple_of(p * 8, 8)
         for yt in range(2):
             own, halo = diffuse(tensor_y(rows[0], yt)), diffuse(tensor_y(rows[1], yt))
             GZ[yt, pl.ds(at, 8), :] = (own + ring_z([own, halo], 0, 1, row)) * z_scale
-        return carry
-    lax.fori_loop(0, 16, face_z, 0)
+    loop(0, 16, face_z, U_FACE)
 
     def keep_z(j, to_left, to_next, source):
         ZA[0, j], ZA[1, j], ZA[2, j] = to_left, to_next, source
@@ -370,17 +405,37 @@
         device_id={"gz": other_core}, device_id_type=MESH)
     cores.start()
 
+    def face_x(p):
+        tiles = tensor_z(tensor_x(0, p), 0)
+        for yt in range(2):
+            BL[p, 0, yt] = diffuse(tensor_y(tiles, yt))
+    loop(0, 17, face_x, U_FACE)
+    last_x = jnp.where(gx == 7, 0.0, 0.5 * STIFFNESS)
+
+    def get_gx(j):
+        return (BL[j, 0, 0:2] + BL[j + 1, 0, 0:2]) * (last_x if j == 15 else 0.5 * STIFFNESS)
+
+    def keep_x(j, to_left, to_next, source):
+        XA[0, j], XA[1, j], XA[2, j] = to_left, to_next, source
+
+    own_x = reduce_block(16, get_gx, lambda j: B[1, :, j], keep_x)
+    for i in range(5):
+        XOWN[i] = own_x[i]
+    pair = pltpu.make_async_remote_copy(
+        src_ref=XOWN, dst_ref=XPEER, send_sem=ss_p, recv_sem=rs_p,
+        device_id={"gx": gx + 1 - 2 * zh}, device_id_type=MESH)
+    pair.start()
+
     y_scale = (jnp.full((8, 128), 0.5 * STIFFNESS, F32),
                jnp.where(jnp.logical_and(lane == 127, gy == 3), 0.0, 0.5 * STIFFNESS).astype(F32))
 
-    def face_y(p, carry):
+    def face_y(p):
         tiles = tensor_z(tensor_x(2, p), 0)
         values = [diffuse(tensor_y(tiles, yt)) for yt in range(3)]
-        at = pl.multiple_of(p * 8, 8)
+        at = p * 8 if isinstance(p, int) else pl.multiple_of(p * 8, 8)
         for yt in range(2):
             GY[yt, pl.ds(at, 8), :] = (values[yt] + ring_y(values, yt, 1, lane)) * y_scale[yt]
-        return carry
-    lax.fori_loop(0, 16, face_y, 0)
+    loop(0, 16, face_y, U_FACE)
 
     cores.wait_recv()
     mine = [PZ[core, i] for i in range(5)]
@@ -415,7 +470,7 @@
 
     for yt in range(2):
         GT[128 * yt:128 * yt + 128, :] = GY[yt].T
-        VT[128 * yt:128 * yt + 128, :] = B[1, 1 + yt, 0:16].reshape(128, 128).T
+        VT[128 * yt:128 * yt + 128, :] = B[1, yt, 0:16].reshape(128, 128).T
 
     def keep_y(j, to_left, to_next, source):
         YA[0, j], YA[1, j], YA[2, j] = to_left, to_next, source
@@ -438,7 +493,6 @@
         y_copy(d).start()
     YG[gy] = PY[...]
 
-    is_solver = jnp.logical_and(zc >= FIRST_SOLVER, zc < FIRST_SOLVER + SOLVERS)
     place = jnp.clip(zc - FIRST_SOLVER, 0, SOLVERS - 1)
 
     def to_chip(p):
@@ -577,13 +631,14 @@
         solved = ZA[2, j] + ZA[0, j] * first + ZA[1, j] * solved
         write(j, solved)
 
-    @pl.when(gx > 0)
-    def _():
-        x_copy(0).wait_send()
-
-    @pl.when(gx < 7)
-    def _():
-        x_copy(1).wait_send()
+    for i, yt in both:
+        @pl.when(sends_x[i])
+        def _():
+            x_first(i, yt).wait_send()
+
+        @pl.when(relays_x[i])
+        def _():
+            x_second(i, yt).wait_send()
     near_send(0)
     near_send(1)
     pair.wait_send()
@@ -609,11 +664,15 @@
     tile = (8, 128)
     dma = pltpu.SemaphoreType.DMA
     vmem = [
-        (3, 4, 27) + tile,
+        (128, 256),
+        (3, 2, 27) + tile,
+        (2, 2) + tile,
+        (3, 2, 2) + tile,
+        (2, 6) + tile,
+        (2, 5) + tile,
         (27, 2, 3) + tile,
         (23, 2, 3) + tile,
         (3, 21, 2, 3) + tile,
-        (16, 2) + tile,
         (2, 128, 128),
         (2, 128, 128),
         (3, 16, 2) + tile,
@@ -638,11 +697,11 @@
         (2, 128, 128),
         (2, 2) + tile,
     ]
-    sems = [(2, 8), (2, 8), (2,), (2,), None, None, (3,), (3,), (3,), (3,), None, None, (4,), (8,), (8,), (4,), None, None]
+    sems = [None, (2, 8), (2, 8), (2, 2), (2, 2), (2, 2), (2, 2), None, None, (3,), (3,), (3,), (3,), None, None, (4,), (8,), (8,), (4,), None, None]
     total = pl.pallas_call(
         kernel,
         out_shape=jax.ShapeDtypeStruct((128, 256), F32),
-        in_specs=[pl.BlockSpec(memory_space=pltpu.VMEM)],
+        in_specs=[pl.BlockSpec(memory_space=pltpu.HBM)],
         out_specs=pl.BlockSpec(memory_space=pltpu.VMEM),
         scratch_shapes=[pltpu.VMEM(shape, F32) for shape in vmem] + [dma(s) if s else dma for s in sems],
         compiler_params=pltpu.CompilerParams(

time: 58.9 us -> 53.8 us (0.913)
  the two profiles are of different devices: /device:TPU:19 before, /device:TPU:15 now
where the time goes in v2:
time: 53.8 us; the launch traced here: 53.7 us
  Pallas kernels  52.1 us (97%)
  local copies, waits for them, and re-layouts  0.9 us (2%)
  other arithmetic  0.67 us (1%)
    pallas_call x1, Pallas kernels, body(): pl.pallas_call(kernel, out_shape=jax.ShapeDtypeStruct((128, 256), F32), i...  52.1 us

profile of v2, /device:TPU:15, one launch (start us, length us, event | category | flops | bytes accessed | tf_op | source)
XLA Modules:
  0.0 53.7 jit_solution(10181471756884472676)
XLA Ops:
  0.0 0.0 copy-start
  0.0 0.9 %copy-done = f32[8,16,256]{2,1,0:T(8,128)S(1)} copy-done((f32[8,16,256]{2,1,0:T(8,128)S(1)}, f32[8,16,256]{2,1,0:T(8,128)}, u32[]{:S(2)}) %copy-start) | copy-done | bytes 131096
  0.9 52.1 %shard_map.17 = f32[128,256]{1,0:T(8,128)S(1)} custom-call(f32[128,256]{1,0:T(8,128)S(1)} %bitcast.2), custom_call_target="tpu_custom_call" | custom-call | flops 40000000 | bytes 262144 | tf_op jit(solution)/shard_map/pallas_call | solution.py:701
  53.0 0.7 %broadcast_multiply_fusion = f32[128,256]{1,0:T(8,128)} fusion(f32[128,256]{1,0:T(8,128)S(1)} %shard_map.17), kind=kLoop, calls=%fused_computation | loop fusion | flops 32768 | bytes 262144 | tf_op jit(solution)/shard_map/div | solution.py:711
Async XLA Ops:
  0.0 0.9 %copy-start = (f32[8,16,256]{2,1,0:T(8,128)S(1)}, f32[8,16,256]{2,1,0:T(8,128)}, u32[]{:S(2)}) copy-start(f32[8,16,256]{2,1,0:T(8,128)} %param.1) | copy-start | bytes 393220

commit v3 on v2

--- a/solution.py
+++ b/solution.py
@@ -14,9 +14,12 @@
 STIFFNESS = 9000.0
 CONTRAST = 0.1
 NEAR = tuple((dz, dy) for dz in (-1, 0, 1) for dy in (-1, 0, 1) if dz or dy)
-SOLVERS = 4
-FIRST_SOLVER = 2
-U_BLUR, U_X, U_SLOPE, U_FACE = 2, 2, 2, 2
+NEAR_HALO = tuple((dz, dy, yt) for yt, dy_end in ((0, -1), (1, 1)) for dz in (-1, 0, 1) for dy in (0, dy_end) if dz or dy)
+SOLVERS = 2
+FIRST_SOLVER = 3
+ROWS = 8 // SOLVERS
+MESSAGE, ANSWER = 10 * ROWS, 4 * ROWS
+U_BLUR, U_X, U_SLOPE, U_FACE = 4, 4, 5, 8
 
 
 def roll_z(tile, j):
@@ -129,8 +132,8 @@
     return source / ground
 
 
-def kernel(v_hbm, o_ref, v_ref, B, HS, HB, RB0, RB1, C, BL, SQ, GZ, GY, XA, XOWN, XPEER, XG, SG, ZA, PZ, ZPEER,
-           MS, ZR, RT, RV, SEP, GT, VT, YA, PY, YG, YS, XY, GIVE, in_sem, ss_h, rs_h, ss_x, rs_x, ss_f, rs_f, ss_p, rs_p,
+def kernel(v_hbm, o_ref, v_ref, B, HS, HB, C, BL, SQ, GZ, GY, XA, XOWN, XPEER, XG, SG, ZA, PZ, ZPEER,
+           MS, ZR, RT, RV, SEP, GT, VT, YA, PY, YG, YS, XY, GIVE, in_sem, ss_h, rs_h, ss_x, rs_x, ss_p, rs_p,
            ss_c, rs_c, ss_y, rs_y, ss_k, rs_k, ss_a, rs_a, ss_r, rs_r, ss_b, rs_b):
     gx, gy, gz = lax.axis_index("gx"), lax.axis_index("gy"), lax.axis_index("gz")
     zc, core = lax.div(gz, 2), lax.rem(gz, 2)
@@ -139,9 +142,6 @@
     load = pltpu.make_async_copy(v_hbm, v_ref, in_sem)
     load.start()
 
-    def chip_at(from_gx, dz):
-        z = lax.rem(lax.rem(from_gx, 2) * 8 + zc + 16 + dz, 16)
-        return lax.div(from_gx, 2) * 2 + lax.div(z, 8), lax.rem(z, 8) * 2 + core
     row = lax.broadcasted_iota(jnp.int32, (8, 128), 0)
     lane = lax.broadcasted_iota(jnp.int32, (8, 128), 1)
 
@@ -150,11 +150,7 @@
         return jnp.logical_and(jnp.logical_and(z >= 0, z < 16), jnp.logical_and(y >= 0, y < 4))
 
     barrier = pltpu.get_barrier_semaphore()
-    above_gx, above_gz = chip_at(gx, 4)
-    below_gx, below_gz = chip_at(gx, -4)
-    via_high = chip_at(gx + 1, 4)
-    via_low = chip_at(jnp.maximum(gx - 1, 0), -4)
-    always = [{"gx": above_gx, "gz": above_gz}, {"gx": below_gx, "gz": below_gz}]
+    always = []
     for d in (2, 4, 6):
         always.append({"gx": lax.rem(gx + d, 8)})
     for d in (1, 2, 3):
@@ -162,15 +158,15 @@
     is_solver = jnp.logical_and(zc >= FIRST_SOLVER, zc < FIRST_SOLVER + SOLVERS)
     total = jnp.int32(len(always))
 
+    @pl.when(gx > 0)
+    def _():
+        pl.semaphore_signal(barrier, inc=1, device_id={"gx": gx - 1}, device_id_type=MESH)
+
     @pl.when(gx < 7)
     def _():
-        pl.semaphore_signal(barrier, inc=1, device_id={"gx": via_high[0], "gz": via_high[1]}, device_id_type=MESH)
-
-    @pl.when(gx > 0)
-    def _():
-        pl.semaphore_signal(barrier, inc=1, device_id={"gx": via_low[0], "gz": via_low[1]}, device_id_type=MESH)
-
-    total = total + jnp.where(below_gx > 0, 1, 0) + jnp.where(above_gx < 7, 1, 0)
+        pl.semaphore_signal(barrier, inc=1, device_id={"gx": gx + 1}, device_id_type=MESH)
+
+    total = total + jnp.where(gx > 0, 1, 0) + jnp.where(gx < 7, 1, 0)
     for target in always:
         pl.semaphore_signal(barrier, inc=1, device_id=target, device_id_type=MESH)
     for p in range(8):
@@ -188,15 +184,13 @@
         def _():
             pl.semaphore_signal(barrier, inc=1, device_id={"gz": gz + dz, "gy": gy + dy}, device_id_type=MESH)
 
-    def pack(phase, layers):
-        low, high = None, None
+    def pack(phase, layers, yt):
+        packed = None
         for i, x in enumerate(layers):
-            a, b = B[1, 0, x], B[1, 1, x]
-            a = pltpu.roll(a, 8 * i, 1) if i else a
-            b = pltpu.roll(b, (8 * i + 8) % 128, 1) if i < 15 else b
-            low = a if low is None else jnp.where(lane < 8 * i, low, a)
-            high = b if high is None else jnp.where(lane < 8 * i, high, b)
-        HS[0, phase], HS[1, phase] = low, high
+            shift = (8 * i + 8 * yt) % 128
+            tile = pltpu.roll(B[1, yt, x], shift, 1) if shift else B[1, yt, x]
+            packed = tile if packed is None else jnp.where(lane < 8 * i, packed, tile)
+        HS[yt, phase] = packed
 
     load.wait()
     for yt in range(2):
@@ -204,7 +198,8 @@
     for x in range(16):
         for yt in range(2):
             B[1, yt, x] = XY[yt, pl.ds(x, 8, stride=16), :]
-    pack(0, range(16))
+    pack(0, range(16), 0)
+    pack(0, range(16), 1)
 
     @pl.when(gz == 0)
     def _():
@@ -238,35 +233,31 @@
 
     pl.semaphore_wait(barrier, total)
 
-    def x_first(i, yt):
-        source, relay, device = ((B.at[1, yt, 0:6], RB0, {"gx": above_gx, "gz": above_gz}),
-                                 (B.at[1, yt, 11:16], RB1, {"gx": below_gx, "gz": below_gz}))[i]
-        return pltpu.make_async_remote_copy(
-            src_ref=source, dst_ref=relay.at[yt], send_sem=ss_f.at[i, yt], recv_sem=rs_f.at[i, yt],
+    def x_copy(i, yt):
+        source, target, device = ((B.at[1, yt, 0:6], B.at[1, yt, 16:22], {"gx": gx - 1}),
+                                  (B.at[1, yt, 11:16], B.at[1, yt, 22:27], {"gx": gx + 1}))[i]
+        return pltpu.make_async_remote_copy(
+            src_ref=source, dst_ref=target, send_sem=ss_x.at[i, yt], recv_sem=rs_x.at[i, yt],
             device_id=device, device_id_type=MESH)
 
-    def x_second(i, yt):
-        relay, target, device = ((RB0, B.at[1, yt, 16:22], {"gx": below_gx - 1, "gz": below_gz}),
-                                 (RB1, B.at[1, yt, 22:27], {"gx": above_gx + 1, "gz": above_gz}))[i]
-        return pltpu.make_async_remote_copy(
-            src_ref=relay.at[yt], dst_ref=target, send_sem=ss_x.at[i, yt], recv_sem=rs_x.at[i, yt],
-            device_id=device, device_id_type=MESH)
-
     sends_x = (gx > 0, gx < 7)
-    relays_x = (below_gx > 0, above_gx < 7)
     gets_x = (gx < 7, gx > 0)
     both = [(i, yt) for yt in range(2) for i in range(2)]
 
     for i, yt in both:
         @pl.when(sends_x[i])
         def _():
-            x_first(i, yt).start()
-
-    def near_copies(phase, i):
-        dz, dy = NEAR[i]
-        xs = slice(0, 16) if phase == 0 else slice(16, 27)
+            x_copy(i, yt).start()
+
+    def near_copy(phase, i):
+        if phase == 0:
+            dz, dy = NEAR[i]
+            ys, xs = slice(0, 2), slice(0, 16)
+        else:
+            dz, dy, yt = NEAR_HALO[i]
+            ys, xs = yt, slice(16, 27)
         if dy == 0:
-            source, target = B.at[1, :, xs], B.at[1 - dz, :, xs]
+            source, target = B.at[1, ys, xs], B.at[1 - dz, ys, xs]
         elif dy == 1:
             source, target = HS.at[1, phase], HB.at[1 - dz, 0, phase]
         else:
@@ -275,31 +266,29 @@
             src_ref=source, dst_ref=target, send_sem=ss_h.at[phase, i], recv_sem=rs_h.at[phase, i],
             device_id={"gz": gz + dz, "gy": gy + dy}, device_id_type=MESH)
 
-    def near_start(phase):
-        for i, (dz, dy) in enumerate(NEAR):
+    def near_list(phase):
+        return [d[:2] for d in (NEAR, NEAR_HALO)[phase]]
+
+    def near_start(phase, first, last):
+        for i, (dz, dy) in enumerate(near_list(phase)):
+            if first <= i < last:
+                @pl.when(inside(dz, dy))
+                def _():
+                    near_copy(phase, i).start()
+
+    def near_recv(phase):
+        for i, (dz, dy) in enumerate(near_list(phase)):
+            @pl.when(inside(-dz, -dy))
+            def _():
+                near_copy(phase, i).wait_recv()
+
+    def near_send(phase):
+        for i, (dz, dy) in enumerate(near_list(phase)):
             @pl.when(inside(dz, dy))
             def _():
-                near_copies(phase, i).start()
-
-    def near_recv(phase):
-        for i, (dz, dy) in enumerate(NEAR):
-            @pl.when(inside(-dz, -dy))
-            def _():
-                near_copies(phase, i).wait_recv()
-
-    def near_send(phase):
-        for i, (dz, dy) in enumerate(NEAR):
-            @pl.when(inside(dz, dy))
-            def _():
-                near_copies(phase, i).wait_send()
-
-    near_start(0)
-
-    for i, yt in both:
-        @pl.when(relays_x[i])
-        def _():
-            x_first(i, yt).wait_recv()
-            x_second(i, yt).start()
+                near_copy(phase, i).wait_send()
+
+    near_start(0, 0, 8)
 
     def blur_zy(xi, phase):
         columns = []
@@ -350,13 +339,13 @@
     loop(5, 17, blur_x, U_X)
     loop(5, 15, slopes, U_SLOPE)
 
-    for i, yt in both:
-        @pl.when(gets_x[i])
-        def _():
-            x_second(i, yt).wait_recv()
-
-    pack(1, range(16, 27))
-    near_start(1)
+    for yt in range(2):
+        for i in range(2):
+            @pl.when(gets_x[i])
+            def _():
+                x_copy(i, yt).wait_recv()
+        pack(1, range(16, 27), yt)
+        near_start(1, 5 * yt, 5 * yt + 5)
     near_recv(1)
     loop(16, 27, lambda xi: blur_zy(xi, 1), U_BLUR)
     loop(0, 5, blur_x, U_X)
@@ -445,17 +434,18 @@
                                       [jnp.where(low, b, a) for a, b in zip(mine, peer)])
     for i in range(5):
         for yt in range(2):
-            MS[pl.ds(2 * i + yt, 8, stride=16), :] = merged_z[i][yt]
+            MS[pl.ds(2 * i + yt, 8, stride=10), :] = merged_z[i][yt]
 
     def to_solver(k):
         return pltpu.make_async_remote_copy(
-            src_ref=MS.at[pl.ds(32 * k, 32)], dst_ref=ZR.at[pl.ds(pl.multiple_of(zc * 32, 32), 32)],
+            src_ref=MS.at[pl.ds(MESSAGE * k, MESSAGE)],
+            dst_ref=ZR.at[pl.ds(pl.multiple_of(zc * MESSAGE, 8), MESSAGE)],
             send_sem=ss_a.at[k], recv_sem=rs_a.at[zc],
             device_id={"gz": 2 * (FIRST_SOLVER + k) + core}, device_id_type=MESH)
 
     def from_chip(p):
         return pltpu.make_async_remote_copy(
-            src_ref=MS.at[pl.ds(0, 32)], dst_ref=ZR.at[pl.ds(32 * p, 32)],
+            src_ref=MS.at[pl.ds(0, MESSAGE)], dst_ref=ZR.at[pl.ds(MESSAGE * p, MESSAGE)],
             send_sem=ss_a.at[0], recv_sem=rs_a.at[p],
             device_id={"gz": other_core}, device_id_type=MESH)
 
@@ -466,7 +456,8 @@
 
         @pl.when(zc == FIRST_SOLVER + k)
         def _():
-            ZR[32 * (FIRST_SOLVER + k):32 * (FIRST_SOLVER + k) + 32, :] = MS[32 * k:32 * k + 32, :]
+            place = MESSAGE * (FIRST_SOLVER + k)
+            ZR[place:place + MESSAGE, :] = MS[MESSAGE * k:MESSAGE * k + MESSAGE, :]
 
     for yt in range(2):
         GT[128 * yt:128 * yt + 128, :] = GY[yt].T
@@ -497,13 +488,14 @@
 
     def to_chip(p):
         return pltpu.make_async_remote_copy(
-            src_ref=RT.at[pl.ds(8 * p, 8)], dst_ref=RV.at[pl.ds(pl.multiple_of(place * 8, 8), 8)],
+            src_ref=RT.at[pl.ds(ANSWER * p, ANSWER)],
+            dst_ref=RV.at[pl.ds(pl.multiple_of(place * ANSWER, 8), ANSWER)],
             send_sem=ss_r.at[p], recv_sem=rs_r.at[place],
             device_id={"gz": 2 * p + core}, device_id_type=MESH)
 
     def from_solver(k):
         return pltpu.make_async_remote_copy(
-            src_ref=RT.at[pl.ds(0, 8)], dst_ref=RV.at[pl.ds(8 * k, 8)],
+            src_ref=RT.at[pl.ds(0, ANSWER)], dst_ref=RV.at[pl.ds(ANSWER * k, ANSWER)],
             send_sem=ss_r.at[0], recv_sem=rs_r.at[k],
             device_id={"gz": other_core}, device_id_type=MESH)
 
@@ -515,14 +507,14 @@
                 from_chip(p).wait_recv()
 
         def gather(i):
-            return jnp.stack([ZR[pl.ds(16 * rr + 2 * i + yt, 8, stride=32), :] for rr in range(2) for yt in range(2)])
+            return jnp.stack([ZR[pl.ds(10 * rr + 2 * i + yt, 8, stride=MESSAGE), :] for rr in range(ROWS) for yt in range(2)])
         series, gl, gr, il, ir = [gather(i) for i in range(5)]
         sigma = ladder_rings(series, gl + pltpu.roll(gr, 1, 1), il + pltpu.roll(ir, 1, 1), 8, 1)
         following = pltpu.roll(sigma, 7, 1)
-        for rr in range(2):
+        for rr in range(ROWS):
             for yt in range(2):
-                RT[pl.ds(4 * rr + yt, 8, stride=8), :] = sigma[2 * rr + yt]
-                RT[pl.ds(4 * rr + 2 + yt, 8, stride=8), :] = following[2 * rr + yt]
+                RT[pl.ds(4 * rr + yt, 8, stride=ANSWER), :] = sigma[2 * rr + yt]
+                RT[pl.ds(4 * rr + 2 + yt, 8, stride=ANSWER), :] = following[2 * rr + yt]
         for p in range(8):
             @pl.when(zc != p)
             def _():
@@ -530,7 +522,7 @@
 
             @pl.when(zc == p)
             def _():
-                RV[pl.ds(pl.multiple_of(place * 8, 8), 8), :] = RT[8 * p:8 * p + 8, :]
+                RV[pl.ds(pl.multiple_of(place * ANSWER, 8), ANSWER), :] = RT[ANSWER * p:ANSWER * p + ANSWER, :]
 
     for d in (1, 2, 3):
         y_back(d).wait_recv()
@@ -634,11 +626,7 @@
     for i, yt in both:
         @pl.when(sends_x[i])
         def _():
-            x_first(i, yt).wait_send()
-
-        @pl.when(relays_x[i])
-        def _():
-            x_second(i, yt).wait_send()
+            x_copy(i, yt).wait_send()
     near_send(0)
     near_send(1)
     pair.wait_send()
@@ -668,8 +656,6 @@
         (3, 2, 27) + tile,
         (2, 2) + tile,
         (3, 2, 2) + tile,
-        (2, 6) + tile,
-        (2, 5) + tile,
         (27, 2, 3) + tile,
         (23, 2, 3) + tile,
         (3, 21, 2, 3) + tile,
@@ -683,9 +669,9 @@
         (3, 8, 2, 16, 128),
         (2, 5, 2) + tile,
         (5, 2) + tile,
-        (128, 128),
-        (256, 128),
-        (64, 128),
+        (80, 128),
+        (8 * MESSAGE, 128),
+        (8 * ANSWER, 128),
         (32, 128),
         (2, 2, 2) + tile,
         (256, 128),
@@ -697,7 +683,7 @@
         (2, 128, 128),
         (2, 2) + tile,
     ]
-    sems = [None, (2, 8), (2, 8), (2, 2), (2, 2), (2, 2), (2, 2), None, None, (3,), (3,), (3,), (3,), None, None, (4,), (8,), (8,), (4,), None, None]
+    sems = [None, (2, 10), (2, 10), (2, 2), (2, 2), None, None, (3,), (3,), (3,), (3,), None, None, (4,), (8,), (8,), (4,), None, None]
     total = pl.pallas_call(
         kernel,
         out_shape=jax.ShapeDtypeStruct((128, 256), F32),

time: 53.8 us -> 51 us (0.948)
  the two profiles are of different devices: /device:TPU:15 before, /device:TPU:88 now
where the time goes in v3:
time: 51 us; the launch traced here: 50.8 us
  Pallas kernels  49.3 us (97%)
  local copies, waits for them, and re-layouts  0.9 us (2%)
  other arithmetic  0.67 us (1%)
    pallas_call x1, Pallas kernels, body(): pl.pallas_call(kernel, out_shape=jax.ShapeDtypeStruct((128, 256), F32), i...  49.3 us

profile of v3, /device:TPU:88, one launch (start us, length us, event | category | flops | bytes accessed | tf_op | source)
XLA Modules:
  0.0 50.8 jit_solution(10495080282959120195)
XLA Ops:
  0.0 0.0 copy-start
  0.0 0.9 %copy-done = f32[8,16,256]{2,1,0:T(8,128)S(1)} copy-done((f32[8,16,256]{2,1,0:T(8,128)S(1)}, f32[8,16,256]{2,1,0:T(8,128)}, u32[]{:S(2)}) %copy-start) | copy-done | bytes 131096
  0.9 49.3 %shard_map.17 = f32[128,256]{1,0:T(8,128)S(1)} custom-call(f32[128,256]{1,0:T(8,128)S(1)} %bitcast.2), custom_call_target="tpu_custom_call" | custom-call | flops 40000000 | bytes 262144 | tf_op jit(solution)/shard_map/pallas_call | solution.py:687
  50.2 0.7 %broadcast_multiply_fusion = f32[128,256]{1,0:T(8,128)} fusion(f32[128,256]{1,0:T(8,128)S(1)} %shard_map.17), kind=kLoop, calls=%fused_computation | loop fusion | flops 32768 | bytes 262144 | tf_op jit(solution)/shard_map/div | solution.py:697
Async XLA Ops:
  0.0 0.9 %copy-start = (f32[8,16,256]{2,1,0:T(8,128)S(1)}, f32[8,16,256]{2,1,0:T(8,128)}, u32[]{:S(2)}) copy-start(f32[8,16,256]{2,1,0:T(8,128)} %param.1) | copy-start | bytes 393220

commit v4 on v3

--- a/solution.py
+++ b/solution.py
@@ -132,9 +132,9 @@
     return source / ground
 
 
-def kernel(v_hbm, o_ref, v_ref, B, HS, HB, C, BL, SQ, GZ, GY, XA, XOWN, XPEER, XG, SG, ZA, PZ, ZPEER,
-           MS, ZR, RT, RV, SEP, GT, VT, YA, PY, YG, YS, XY, GIVE, in_sem, ss_h, rs_h, ss_x, rs_x, ss_p, rs_p,
-           ss_c, rs_c, ss_y, rs_y, ss_k, rs_k, ss_a, rs_a, ss_r, rs_r, ss_b, rs_b):
+def kernel(v_hbm, o_ref, v_ref, B, HS, HB, C, BL, SQ, GX, GZ, GY, XA, XOWN, XPEER, XG, SG, ZA, PZ, ZPEER,
+           MS, ZR, RT, RV, GT, VT, YA, PY, YG, YS, XY, in_sem, ss_h, rs_h, ss_x, rs_x, ss_p, rs_p,
+           ss_c, rs_c, ss_y, rs_y, ss_k, rs_k, ss_a, rs_a, ss_r, rs_r):
     gx, gy, gz = lax.axis_index("gx"), lax.axis_index("gy"), lax.axis_index("gz")
     zc, core = lax.div(gz, 2), lax.rem(gz, 2)
     xc, zh = lax.div(gx, 2), lax.rem(gx, 2)
@@ -320,24 +320,31 @@
     y_one = jnp.where(lane < 64, right, left).astype(F32)
     halves = [[z_half[0], z_half[0], z_half[0] * y_one], [z_half[1], z_half[1], z_half[1] * y_one]]
 
-    def slopes(p):
+    def slopes(p, axes):
         x_in = jnp.where(jnp.logical_or(jnp.logical_and(p < 2, gx == 0), jnp.logical_and(p > 17, gx == 7)), 0.0, 1.0)
         tiles = [[BL[p + 1, zt, yt] for yt in range(3)] for zt in range(2)]
         for zt in range(2):
             for yt in range(3):
                 half = halves[zt][yt] * x_in
-                slope_x = (BL[p + 2, zt, yt] - BL[p, zt, yt]) * half
-                SQ[0, p, zt, yt] = slope_x * slope_x
-                column = [tiles[0][yt], tiles[1][yt]]
-                slope_z = (ring_z(column, zt, 1, row) - ring_z(column, zt, -1, row)) * half
-                SQ[1, p, zt, yt] = slope_z * slope_z
-                slope_y = (ring_y(tiles[zt], yt, 1, lane) - ring_y(tiles[zt], yt, -1, lane)) * half
-                SQ[2, p, zt, yt] = slope_y * slope_y
+                for axis in axes:
+                    if axis == 0:
+                        change = BL[p + 2, zt, yt] - BL[p, zt, yt]
+                    elif axis == 1:
+                        column = [tiles[0][yt], tiles[1][yt]]
+                        change = ring_z(column, zt, 1, row) - ring_z(column, zt, -1, row)
+                    else:
+                        change = ring_y(tiles[zt], yt, 1, lane) - ring_y(tiles[zt], yt, -1, lane)
+                    slope = change * half
+                    SQ[axis, p, zt, yt] = slope * slope
+
+    def outer_slopes(axis):
+        loop(0, 5, lambda p: slopes(p, (axis,)), 5)
+        loop(15, 21, lambda p: slopes(p, (axis,)), 6)
 
     near_recv(0)
     loop(0, 16, lambda xi: blur_zy(xi, 0), U_BLUR)
     loop(5, 17, blur_x, U_X)
-    loop(5, 15, slopes, U_SLOPE)
+    loop(5, 15, lambda p: slopes(p, (0, 1, 2)), U_SLOPE)
 
     for yt in range(2):
         for i in range(2):
@@ -350,8 +357,7 @@
     loop(16, 27, lambda xi: blur_zy(xi, 1), U_BLUR)
     loop(0, 5, blur_x, U_X)
     loop(17, 23, blur_x, U_X)
-    loop(0, 5, slopes, U_SLOPE)
-    loop(15, 21, slopes, U_SLOPE)
+    outer_slopes(0)
 
     def diffuse(tensor):
         return 1.0 / (1.0 + tensor * (1.0 / (CONTRAST * CONTRAST)))
@@ -364,6 +370,36 @@
 
     def tensor_y(tiles, yt):
         return taps_sum([ring_y(tiles, yt, j, lane) for j in range(-2, 3)])
+
+    def face_x(p):
+        tiles = tensor_z(tensor_x(0, p), 0)
+        for yt in range(2):
+            GX[p, yt] = diffuse(tensor_y(tiles, yt))
+    loop(0, 17, face_x, U_FACE)
+    last_x = jnp.where(gx == 7, 0.0, 0.5 * STIFFNESS)
+
+    def get_gx(j):
+        return (GX[j] + GX[j + 1]) * (last_x if j == 15 else 0.5 * STIFFNESS)
+
+    def keep_x(j, to_left, to_next, source):
+        XA[0, j], XA[1, j], XA[2, j] = to_left, to_next, source
+
+    def halves_of(get):
+        return lambda j: jnp.stack([get(j), get(j + 8)])
+
+    halved = reduce_block(8, halves_of(get_gx), halves_of(lambda j: B[1, :, j]), keep_x)
+    own_x, middle_own = merge_blocks([part[0] for part in halved], [part[1] for part in halved])
+    for i in range(5):
+        for yt in range(2):
+            XOWN[yt, i] = own_x[i][yt]
+
+    def pair(yt):
+        return pltpu.make_async_remote_copy(
+            src_ref=XOWN.at[yt], dst_ref=XPEER.at[yt], send_sem=ss_p.at[yt], recv_sem=rs_p.at[yt],
+            device_id={"gx": gx + 1 - 2 * zh}, device_id_type=MESH)
+
+    for yt in range(2):
+        pair(yt).start()
 
     z_scale = jnp.where(jnp.logical_and(row == 7, gz == 15), 0.0, 0.5 * STIFFNESS).astype(F32)
 
@@ -374,6 +410,7 @@
         for yt in range(2):
             own, halo = diffuse(tensor_y(rows[0], yt)), diffuse(tensor_y(rows[1], yt))
             GZ[yt, pl.ds(at, 8), :] = (own + ring_z([own, halo], 0, 1, row)) * z_scale
+    outer_slopes(1)
     loop(0, 16, face_z, U_FACE)
 
     def keep_z(j, to_left, to_next, source):
@@ -390,30 +427,9 @@
         for h in range(2):
             PZ[h, i] = own_z[i][:, 8 * h:8 * h + 8, :]
     cores = pltpu.make_async_remote_copy(
-        src_ref=PZ.at[1 - core], dst_ref=ZPEER, send_sem=ss_k, recv_sem=rs_k,
+        src_ref=PZ, dst_ref=ZPEER, send_sem=ss_k, recv_sem=rs_k,
         device_id={"gz": other_core}, device_id_type=MESH)
     cores.start()
-
-    def face_x(p):
-        tiles = tensor_z(tensor_x(0, p), 0)
-        for yt in range(2):
-            BL[p, 0, yt] = diffuse(tensor_y(tiles, yt))
-    loop(0, 17, face_x, U_FACE)
-    last_x = jnp.where(gx == 7, 0.0, 0.5 * STIFFNESS)
-
-    def get_gx(j):
-        return (BL[j, 0, 0:2] + BL[j + 1, 0, 0:2]) * (last_x if j == 15 else 0.5 * STIFFNESS)
-
-    def keep_x(j, to_left, to_next, source):
-        XA[0, j], XA[1, j], XA[2, j] = to_left, to_next, source
-
-    own_x = reduce_block(16, get_gx, lambda j: B[1, :, j], keep_x)
-    for i in range(5):
-        XOWN[i] = own_x[i]
-    pair = pltpu.make_async_remote_copy(
-        src_ref=XOWN, dst_ref=XPEER, send_sem=ss_p, recv_sem=rs_p,
-        device_id={"gx": gx + 1 - 2 * zh}, device_id_type=MESH)
-    pair.start()
 
     y_scale = (jnp.full((8, 128), 0.5 * STIFFNESS, F32),
                jnp.where(jnp.logical_and(lane == 127, gy == 3), 0.0, 0.5 * STIFFNESS).astype(F32))
@@ -424,14 +440,19 @@
         at = p * 8 if isinstance(p, int) else pl.multiple_of(p * 8, 8)
         for yt in range(2):
             GY[yt, pl.ds(at, 8), :] = (values[yt] + ring_y(values, yt, 1, lane)) * y_scale[yt]
+    outer_slopes(2)
     loop(0, 16, face_y, U_FACE)
 
     cores.wait_recv()
-    mine = [PZ[core, i] for i in range(5)]
-    peer = [ZPEER[i] for i in range(5)]
     low = core == 0
-    merged_z, middle_z = merge_blocks([jnp.where(low, a, b) for a, b in zip(mine, peer)],
-                                      [jnp.where(low, b, a) for a, b in zip(mine, peer)])
+
+    def merge_cores(half):
+        mine = [PZ[half, i] for i in range(5)]
+        peer = [ZPEER[half, i] for i in range(5)]
+        return merge_blocks([jnp.where(low, a, b) for a, b in zip(mine, peer)],
+                            [jnp.where(low, b, a) for a, b in zip(mine, peer)])
+
+    merged_z = merge_cores(core)[0]
     for i in range(5):
         for yt in range(2):
             MS[pl.ds(2 * i + yt, 8, stride=10), :] = merged_z[i][yt]
@@ -486,18 +507,21 @@
 
     place = jnp.clip(zc - FIRST_SOLVER, 0, SOLVERS - 1)
 
-    def to_chip(p):
+    def to_chip(p, side):
         return pltpu.make_async_remote_copy(
             src_ref=RT.at[pl.ds(ANSWER * p, ANSWER)],
-            dst_ref=RV.at[pl.ds(pl.multiple_of(place * ANSWER, 8), ANSWER)],
-            send_sem=ss_r.at[p], recv_sem=rs_r.at[place],
-            device_id={"gz": 2 * p + core}, device_id_type=MESH)
-
-    def from_solver(k):
-        return pltpu.make_async_remote_copy(
-            src_ref=RT.at[pl.ds(0, ANSWER)], dst_ref=RV.at[pl.ds(ANSWER * k, ANSWER)],
-            send_sem=ss_r.at[0], recv_sem=rs_r.at[k],
+            dst_ref=RV.at[pl.ds(pl.multiple_of((core * SOLVERS + place) * ANSWER, 8), ANSWER)],
+            send_sem=ss_r.at[side, p], recv_sem=rs_r.at[core * SOLVERS + place],
+            device_id={"gz": 2 * p + (1 - core if side else core)}, device_id_type=MESH)
+
+    def from_solver(half, k):
+        at = half * SOLVERS + k
+        return pltpu.make_async_remote_copy(
+            src_ref=RT.at[pl.ds(0, ANSWER)], dst_ref=RV.at[pl.ds(ANSWER * at, ANSWER)],
+            send_sem=ss_r.at[0, 0], recv_sem=rs_r.at[at],
             device_id={"gz": other_core}, device_id_type=MESH)
+
+    far_first = sorted(range(8), key=lambda p: -abs(2 * p - 7))
 
     @pl.when(is_solver)
     def _():
@@ -515,14 +539,17 @@
             for yt in range(2):
                 RT[pl.ds(4 * rr + yt, 8, stride=ANSWER), :] = sigma[2 * rr + yt]
                 RT[pl.ds(4 * rr + 2 + yt, 8, stride=ANSWER), :] = following[2 * rr + yt]
-        for p in range(8):
+        for p in far_first:
+            to_chip(p, 1).start()
+
             @pl.when(zc != p)
             def _():
-                to_chip(p).start()
+                to_chip(p, 0).start()
 
             @pl.when(zc == p)
             def _():
-                RV[pl.ds(pl.multiple_of(place * ANSWER, 8), ANSWER), :] = RT[ANSWER * p:ANSWER * p + ANSWER, :]
+                at = pl.multiple_of((core * SOLVERS + place) * ANSWER, 8)
+                RV[pl.ds(at, ANSWER), :] = RT[ANSWER * p:ANSWER * p + ANSWER, :]
 
     for d in (1, 2, 3):
         y_back(d).wait_recv()
@@ -538,58 +565,62 @@
     for yt in range(2):
         XY[yt] = VT[128 * yt:128 * yt + 128, :].T
 
-    pair.wait_recv()
-    mine = [XOWN[i] for i in range(5)]
-    peer = [XPEER[i] for i in range(5)]
     low_x = zh == 0
-    merged_x, middle_x = merge_blocks([jnp.where(low_x, a, b) for a, b in zip(mine, peer)],
-                                      [jnp.where(low_x, b, a) for a, b in zip(mine, peer)])
-    for i in range(5):
-        XG[xc, i] = merged_x[i]
-
-    def xg_copy(d):
-        return pltpu.make_async_remote_copy(
-            src_ref=XG.at[xc], dst_ref=XG.at[xc], send_sem=ss_c.at[d - 1], recv_sem=rs_c.at[d - 1],
+
+    def xg_copy(yt, d):
+        return pltpu.make_async_remote_copy(
+            src_ref=XG.at[xc, yt], dst_ref=XG.at[xc, yt], send_sem=ss_c.at[yt, d - 1], recv_sem=rs_c.at[yt, d - 1],
             device_id={"gx": lax.rem(gx + 2 * d, 8)}, device_id_type=MESH)
 
-    def xg_back(d):
-        return pltpu.make_async_remote_copy(
-            src_ref=XG.at[xc], dst_ref=XG.at[lax.rem(xc + 4 - d, 4)], send_sem=ss_c.at[d - 1], recv_sem=rs_c.at[d - 1],
+    def xg_back(yt, d):
+        return pltpu.make_async_remote_copy(
+            src_ref=XG.at[xc, yt], dst_ref=XG.at[lax.rem(xc + 4 - d, 4), yt],
+            send_sem=ss_c.at[yt, d - 1], recv_sem=rs_c.at[yt, d - 1],
             device_id={"gx": lax.rem(gx + 2 * d, 8)}, device_id_type=MESH)
 
-    for d in (1, 2, 3):
-        xg_copy(d).start()
-
-    for k in range(SOLVERS):
-        @pl.when(zc != FIRST_SOLVER + k)
-        def _():
-            from_solver(k).wait_recv()
-
-    def ends(w):
-        return jnp.stack([RV[pl.ds(2 * w + yt, 8, stride=4), :] for yt in range(2)])
-    start, end = ends(0), ends(1)
-    middle = middle_z[2] + middle_z[0] * start + middle_z[1] * end
-    SEP[core, 0] = jnp.where(low, start, middle)
-    SEP[core, 1] = jnp.where(low, middle, end)
-    GIVE[0] = jnp.where(low, middle, start)
-    GIVE[1] = jnp.where(low, end, middle)
-    give = pltpu.make_async_remote_copy(
-        src_ref=GIVE, dst_ref=SEP.at[core], send_sem=ss_b, recv_sem=rs_b,
-        device_id={"gz": other_core}, device_id_type=MESH)
-    give.start()
-
-    for d in (1, 2, 3):
-        xg_back(d).wait_recv()
-    ground, source = XG[0, 1], XG[0, 3]
+    middles = []
+    for yt in range(2):
+        pair(yt).wait_recv()
+        mine = [XOWN[yt, i] for i in range(5)]
+        peer = [XPEER[yt, i] for i in range(5)]
+        merged_x, middle = merge_blocks([jnp.where(low_x, a, b) for a, b in zip(mine, peer)],
+                                        [jnp.where(low_x, b, a) for a, b in zip(mine, peer)])
+        middles.append(middle)
+        for i in range(5):
+            XG[xc, yt, i] = merged_x[i]
+        for d in (1, 2, 3):
+            xg_copy(yt, d).start()
+    middle_x = [jnp.stack(part) for part in zip(*middles)]
+
+    middles_z = [merge_cores(half)[1] for half in range(2)]
+    for half in range(2):
+        for k in range(SOLVERS):
+            @pl.when(jnp.logical_or(zc != FIRST_SOLVER + k, core != half))
+            def _():
+                from_solver(half, k).wait_recv()
+
+    first_z, next_z = [], []
+    for half in range(2):
+        start, end = [jnp.stack([RV[pl.ds(4 * 8 * half + 2 * w + yt, 8, stride=4), :] for yt in range(2)])
+                      for w in range(2)]
+        to_l, to_r, source = middles_z[half]
+        middle = source + to_l * start + to_r * end
+        first_z.append(jnp.where(low, start, middle))
+        next_z.append(jnp.where(low, middle, end))
+
+    for yt in range(2):
+        for d in (1, 2, 3):
+            xg_back(yt, d).wait_recv()
+    ground, source = XG[0, :, 1], XG[0, :, 3]
     stack = []
     for p in range(4):
-        series = XG[p, 0]
+        series = XG[p, :, 0]
         inverse = 1.0 / (ground + series)
         ratio = series * inverse
         stack.append((source * inverse, ratio))
         if p < 3:
-            ground = XG[p + 1, 1] + XG[p, 2] + ratio * ground
-            source = XG[p + 1, 3] + XG[p, 4] + ratio * source
+            ground = XG[p + 1, :, 1] + XG[p, :, 2] + ratio * ground
+            source = XG[p + 1, :, 3] + XG[p, :, 4] + ratio * source
     value = stack[3][0]
     SG[4] = jnp.zeros((2, 8, 128), F32)
     SG[3] = value
@@ -599,21 +630,21 @@
     start_x, end_x = SG[xc], SG[xc + 1]
     middle_node = middle_x[2] + middle_x[0] * start_x + middle_x[1] * end_x
     first = jnp.where(low_x, start_x, middle_node)
-    solved = jnp.where(low_x, middle_node, end_x)
+    end_own = jnp.where(low_x, middle_node, end_x)
+    middle_block = middle_own[2] + middle_own[0] * first + middle_own[1] * end_own
+    first, solved = jnp.stack([first, middle_block]), jnp.stack([middle_block, end_own])
 
     def add_x(j, value):
-        for yt in range(2):
-            XY[yt, 8 * j:8 * j + 8, :] = XY[yt, 8 * j:8 * j + 8, :] + value[yt]
+        for half in range(2):
+            at = 64 * half + 8 * j
+            for yt in range(2):
+                XY[yt, at:at + 8, :] = XY[yt, at:at + 8, :] + value[half, yt]
     add_x(0, first)
-    for j in range(15, 0, -1):
+    for j in range(7, 0, -1):
         solved = XA[2, j] + XA[0, j] * first + XA[1, j] * solved
         add_x(j, solved)
 
-    pltpu.make_async_remote_copy(
-        src_ref=GIVE, dst_ref=SEP.at[1 - core], send_sem=ss_b, recv_sem=rs_b,
-        device_id={"gz": other_core}, device_id_type=MESH).wait_recv()
-    first = jnp.concatenate([SEP[0, 0], SEP[1, 0]], axis=1)
-    solved = jnp.concatenate([SEP[0, 1], SEP[1, 1]], axis=1)
+    first, solved = jnp.concatenate(first_z, axis=1), jnp.concatenate(next_z, axis=1)
 
     def write(j, value):
         for yt in range(2):
@@ -629,10 +660,12 @@
             x_copy(i, yt).wait_send()
     near_send(0)
     near_send(1)
-    pair.wait_send()
+    for yt in range(2):
+        pair(yt).wait_send()
+        for d in (1, 2, 3):
+            xg_copy(yt, d).wait_send()
     for d in (1, 2, 3):
         y_copy(d).wait_send()
-        xg_copy(d).wait_send()
     for k in range(SOLVERS):
         @pl.when(zc != FIRST_SOLVER + k)
         def _():
@@ -641,11 +674,12 @@
     @pl.when(is_solver)
     def _():
         for p in range(8):
+            to_chip(p, 1).wait_send()
+
             @pl.when(zc != p)
             def _():
-                to_chip(p).wait_send()
+                to_chip(p, 0).wait_send()
     cores.wait_send()
-    give.wait_send()
 
 
 def body(volume):
@@ -659,21 +693,21 @@
         (27, 2, 3) + tile,
         (23, 2, 3) + tile,
         (3, 21, 2, 3) + tile,
+        (17, 2) + tile,
         (2, 128, 128),
         (2, 128, 128),
-        (3, 16, 2) + tile,
-        (5, 2) + tile,
-        (5, 2) + tile,
-        (4, 5, 2) + tile,
+        (3, 8, 2, 2) + tile,
+        (2, 5) + tile,
+        (2, 5) + tile,
+        (4, 2, 5) + tile,
         (5, 2) + tile,
         (3, 8, 2, 16, 128),
         (2, 5, 2) + tile,
-        (5, 2) + tile,
+        (2, 5, 2) + tile,
         (80, 128),
         (8 * MESSAGE, 128),
         (8 * ANSWER, 128),
-        (32, 128),
-        (2, 2, 2) + tile,
+        (64, 128),
         (256, 128),
         (256, 128),
         (3, 32) + tile,
@@ -681,9 +715,8 @@
         (4, 5) + tile,
         (2, 4) + tile,
         (2, 128, 128),
-        (2, 2) + tile,
     ]
-    sems = [None, (2, 10), (2, 10), (2, 2), (2, 2), None, None, (3,), (3,), (3,), (3,), None, None, (4,), (8,), (8,), (4,), None, None]
+    sems = [None, (2, 10), (2, 10), (2, 2), (2, 2), (2,), (2,), (2, 3), (2, 3), (3,), (3,), None, None, (SOLVERS,), (8,), (2, 8), (2 * SOLVERS,)]
     total = pl.pallas_call(
         kernel,
         out_shape=jax.ShapeDtypeStruct((128, 256), F32),

time: 51 us -> 49.3 us (0.967)
  Pallas kernels: 49.3 us -> 47.6 us
    pallas_call x1, Pallas kernels: 49.3 us -> 47.6 us  [body(): pl.pallas_call(kernel, out_shape=jax.ShapeDtypeStruct((128, 256), F32), i...]
where the time goes in v4:
time: 49.3 us; the launch traced here: 49.1 us
  Pallas kernels  47.6 us (97%)
  local copies, waits for them, and re-layouts  0.9 us (2%)
  other arithmetic  0.67 us (1%)
    pallas_call x1, Pallas kernels, body(): pl.pallas_call(kernel, out_shape=jax.ShapeDtypeStruct((128, 256), F32), i...  47.6 us

profile of v4, /device:TPU:88, one launch (start us, length us, event | category | flops | bytes accessed | tf_op | source)
XLA Modules:
  0.0 49.1 jit_solution(15610956013828540795)
XLA Ops:
  0.0 0.0 copy-start
  0.0 0.9 %copy-done = f32[8,16,256]{2,1,0:T(8,128)S(1)} copy-done((f32[8,16,256]{2,1,0:T(8,128)S(1)}, f32[8,16,256]{2,1,0:T(8,128)}, u32[]{:S(2)}) %copy-start) | copy-done | bytes 131096
  0.9 47.6 %shard_map.17 = f32[128,256]{1,0:T(8,128)S(1)} custom-call(f32[128,256]{1,0:T(8,128)S(1)} %bitcast.2), custom_call_target="tpu_custom_call" | custom-call | flops 40000000 | bytes 262144 | tf_op jit(solution)/shard_map/pallas_call | solution.py:720
  48.5 0.7 %broadcast_multiply_fusion = f32[128,256]{1,0:T(8,128)} fusion(f32[128,256]{1,0:T(8,128)S(1)} %shard_map.17), kind=kLoop, calls=%fused_computation | loop fusion | flops 32768 | bytes 262144 | tf_op jit(solution)/shard_map/div | solution.py:730
Async XLA Ops:
  0.0 0.9 %copy-start = (f32[8,16,256]{2,1,0:T(8,128)S(1)}, f32[8,16,256]{2,1,0:T(8,128)}, u32[]{:S(2)}) copy-start(f32[8,16,256]{2,1,0:T(8,128)} %param.1) | copy-start | bytes 393220

commit v5 on v4

--- a/solution.py
+++ b/solution.py
@@ -80,6 +80,13 @@
         step(i)
 
 
+def reciprocal(value):
+    guess = pl.reciprocal(value, approx=True)
+    for _ in range(1):
+        guess = guess * (2.0 - value * guess)
+    return guess
+
+
 def reduce_block(count, get_face, get_value, keep):
     series = get_face(0)
     left_ground = jnp.ones_like(series)
@@ -88,7 +95,7 @@
     source = get_value(1)
     for j in range(1, count):
         face = get_face(j)
-        inverse = 1.0 / (series + ground + face)
+        inverse = reciprocal(series + ground + face)
         to_left, to_next = series * inverse, face * inverse
         keep(j, to_left, to_next, source * inverse)
         left_ground = left_ground + to_left * ground
@@ -104,7 +111,7 @@
     a_l, gl_l, gr_l, il_l, ir_l = left
     a_r, gl_r, gr_r, il_r, ir_r = right
     ground, source = gr_l + gl_r, ir_l + il_r
-    inverse = 1.0 / (a_l + ground + a_r)
+    inverse = reciprocal(a_l + ground + a_r)
     to_l, to_r = a_l * inverse, a_r * inverse
     merged = (to_l * a_r, gl_l + to_l * ground, gr_r + to_r * ground, il_l + to_l * source, ir_r + to_r * source)
     return merged, (to_l, to_r, source * inverse)
@@ -121,7 +128,7 @@
             return pltpu.roll(array, size - step, axis)
 
         before = low(series)
-        inverse = 1.0 / (ground + series + before)
+        inverse = reciprocal(ground + series + before)
         from_low, from_high = before * low(inverse), series * high(inverse)
         ground, source, series = (
             ground + from_low * low(ground) + from_high * high(ground),
@@ -129,7 +136,7 @@
             from_high * high(series),
         )
         step *= 2
-    return source / ground
+    return source * reciprocal(ground)
 
 
 def kernel(v_hbm, o_ref, v_ref, B, HS, HB, C, BL, SQ, GX, GZ, GY, XA, XOWN, XPEER, XG, SG, ZA, PZ, ZPEER,
@@ -360,7 +367,7 @@
     outer_slopes(0)
 
     def diffuse(tensor):
-        return 1.0 / (1.0 + tensor * (1.0 / (CONTRAST * CONTRAST)))
+        return reciprocal(1.0 + tensor * (1.0 / (CONTRAST * CONTRAST)))
 
     def tensor_x(a, p):
         return [[taps_sum([SQ[a, p + j, zt, yt] for j in range(5)]) for yt in range(3)] for zt in range(2)]
@@ -550,6 +557,33 @@
             def _():
                 at = pl.multiple_of((core * SOLVERS + place) * ANSWER, 8)
                 RV[pl.ds(at, ANSWER), :] = RT[ANSWER * p:ANSWER * p + ANSWER, :]
+
+    low_x = zh == 0
+
+    def xg_copy(yt, d):
+        return pltpu.make_async_remote_copy(
+            src_ref=XG.at[xc, yt], dst_ref=XG.at[xc, yt], send_sem=ss_c.at[yt, d - 1], recv_sem=rs_c.at[yt, d - 1],
+            device_id={"gx": lax.rem(gx + 2 * d, 8)}, device_id_type=MESH)
+
+    def xg_back(yt, d):
+        return pltpu.make_async_remote_copy(
+            src_ref=XG.at[xc, yt], dst_ref=XG.at[lax.rem(xc + 4 - d, 4), yt],
+            send_sem=ss_c.at[yt, d - 1], recv_sem=rs_c.at[yt, d - 1],
+            device_id={"gx": lax.rem(gx + 2 * d, 8)}, device_id_type=MESH)
+
+    middles = []
+    for yt in range(2):
+        pair(yt).wait_recv()
+        mine = [XOWN[yt, i] for i in range(5)]
+        peer = [XPEER[yt, i] for i in range(5)]
+        merged_x, middle = merge_blocks([jnp.where(low_x, a, b) for a, b in zip(mine, peer)],
+                                        [jnp.where(low_x, b, a) for a, b in zip(mine, peer)])
+        middles.append(middle)
+        for i in range(5):
+            XG[xc, yt, i] = merged_x[i]
+        for d in (2, 1, 3):
+            xg_copy(yt, d).start()
+    middle_x = [jnp.stack(part) for part in zip(*middles)]
 
     for d in (1, 2, 3):
         y_back(d).wait_recv()
@@ -565,33 +599,6 @@
     for yt in range(2):
         XY[yt] = VT[128 * yt:128 * yt + 128, :].T
 
-    low_x = zh == 0
-
-    def xg_copy(yt, d):
-        return pltpu.make_async_remote_copy(
-            src_ref=XG.at[xc, yt], dst_ref=XG.at[xc, yt], send_sem=ss_c.at[yt, d - 1], recv_sem=rs_c.at[yt, d - 1],
-            device_id={"gx": lax.rem(gx + 2 * d, 8)}, device_id_type=MESH)
-
-    def xg_back(yt, d):
-        return pltpu.make_async_remote_copy(
-            src_ref=XG.at[xc, yt], dst_ref=XG.at[lax.rem(xc + 4 - d, 4), yt],
-            send_sem=ss_c.at[yt, d - 1], recv_sem=rs_c.at[yt, d - 1],
-            device_id={"gx": lax.rem(gx + 2 * d, 8)}, device_id_type=MESH)
-
-    middles = []
-    for yt in range(2):
-        pair(yt).wait_recv()
-        mine = [XOWN[yt, i] for i in range(5)]
-        peer = [XPEER[yt, i] for i in range(5)]
-        merged_x, middle = merge_blocks([jnp.where(low_x, a, b) for a, b in zip(mine, peer)],
-                                        [jnp.where(low_x, b, a) for a, b in zip(mine, peer)])
-        middles.append(middle)
-        for i in range(5):
-            XG[xc, yt, i] = merged_x[i]
-        for d in (1, 2, 3):
-            xg_copy(yt, d).start()
-    middle_x = [jnp.stack(part) for part in zip(*middles)]
-
     middles_z = [merge_cores(half)[1] for half in range(2)]
     for half in range(2):
         for k in range(SOLVERS):
@@ -615,7 +622,7 @@
     stack = []
     for p in range(4):
         series = XG[p, :, 0]
-        inverse = 1.0 / (ground + series)
+        inverse = reciprocal(ground + series)
         ratio = series * inverse
         stack.append((source * inverse, ratio))
         if p < 3:

time: 49.3 us -> 49.1 us (level)
  no operation moved by 1% of the time
where the time goes in v5:
time: 49.1 us; the launch traced here: 49 us
  Pallas kernels  47.4 us (97%)
  local copies, waits for them, and re-layouts  0.9 us (2%)
  other arithmetic  0.67 us (1%)
    pallas_call x1, Pallas kernels, body(): pl.pallas_call(kernel, out_shape=jax.ShapeDtypeStruct((128, 256), F32), i...  47.4 us

profile of v5, /device:TPU:88, one launch (start us, length us, event | category | flops | bytes accessed | tf_op | source)
XLA Modules:
  0.0 49.0 jit_solution(17740598318646899787)
XLA Ops:
  0.0 0.0 copy-start
  0.0 0.9 %copy-done = f32[8,16,256]{2,1,0:T(8,128)S(1)} copy-done((f32[8,16,256]{2,1,0:T(8,128)S(1)}, f32[8,16,256]{2,1,0:T(8,128)}, u32[]{:S(2)}) %copy-start) | copy-done | bytes 131096
  0.9 47.4 %shard_map.17 = f32[128,256]{1,0:T(8,128)S(1)} custom-call(f32[128,256]{1,0:T(8,128)S(1)} %bitcast.2), custom_call_target="tpu_custom_call" | custom-call | flops 40000000 | bytes 262144 | tf_op jit(solution)/shard_map/pallas_call | solution.py:727
  48.3 0.7 %broadcast_multiply_fusion = f32[128,256]{1,0:T(8,128)} fusion(f32[128,256]{1,0:T(8,128)S(1)} %shard_map.17), kind=kLoop, calls=%fused_computation | loop fusion | flops 32768 | bytes 262144 | tf_op jit(solution)/shard_map/div | solution.py:737
Async XLA Ops:
  0.0 0.9 %copy-start = (f32[8,16,256]{2,1,0:T(8,128)S(1)}, f32[8,16,256]{2,1,0:T(8,128)}, u32[]{:S(2)}) copy-start(f32[8,16,256]{2,1,0:T(8,128)} %param.1) | copy-start | bytes 393220
